TPU v7x, 512 devices: a whole 4x4x16 slice. The times are simulated.
512 devices in a mesh: freq: 32 (over z_hi, y, core), gx: 16 (over z_lo, x).
Axes of the slice: x: 4, y: 4, z: 16 (z_hi: 4, z_lo: 4; z = z_hi * 4 + z_lo), core: 2. Of those that a mesh axis runs over, the one named last changes fastest.
Arguments:
- wavefield: float32 [2, 64, 2048, 128], P(None, 'freq', 'gx'), may hold values from -6 to 6
- velocity_bank: float32 [32, 2048, 128], P('freq', 'gx'), may hold values from 1.5 to 4.5
- owner: int32 [1], replicated, may hold values from 0 to 31
Outputs:
- wave_out: float32 [2, 64, 2048, 128], P(None, 'freq', 'gx')
- stacked_image: float32 [2048, 128], P('gx')
All inputs are finite; a program needn't handle non-finite values.
Results may differ from a plain program's by a relative error of at most 0.0015.
Values sent between devices are 32-bit elements; how exact they have to be, the bound alone decides.
No kernel may reach another device: no remote copies, remote signals or barrier semaphores. Data moves between devices by JAX's collectives and lax.ppermute only.
A program may use at most 64 MiB of HBM per device.

v0:
```python
import math

import jax
import jax.numpy as jnp
from jax import lax
from jax.sharding import PartitionSpec as P

BETA = 1.0 / 6.0
GAIN = 30000.0
PHASE = 2.0


def shifted(block, axis, distance):
    devices = range(lax.axis_size(axis))
    route = [(i - distance, i) for i in devices if i - distance in devices]
    return lax.ppermute(block, axis, route)


def padded_2(block, sides, width):
    for axis, dim in sides:
        count = lax.axis_size(axis)
        forward = [(i, i + 1) for i in range(count - 1)]
        backward = [(target, source) for source, target in forward]
        low = lax.ppermute(
            lax.slice_in_dim(block, block.shape[dim] - width, None, axis=dim), axis, forward
        )
        high = lax.ppermute(lax.slice_in_dim(block, 0, width, axis=dim), axis, backward)
        block = jnp.concatenate([low, block, high], axis=dim)
    return block


def broadcast(value, axis, source):
    kept = jnp.where(lax.axis_index(axis) == source, value, 0).astype(value.dtype)
    return lax.psum(kept, axis)


def times_complex(left_re, left_im, right_re, right_im):
    return (left_re * right_re - left_im * right_im, left_re * right_im + left_im * right_re)


def divide_complex(top_re, top_im, bottom_re, bottom_im):
    denominator = bottom_re * bottom_re + bottom_im * bottom_im
    return (
        (top_re * bottom_re + top_im * bottom_im) / denominator,
        (top_im * bottom_re - top_re * bottom_im) / denominator,
    )


def pack_system(members):
    return jnp.stack([jnp.stack([member[0], member[1]]) for member in members])


def build(wave_in, kappa_re, kappa_im, prev_rows, next_rows, head_mask, tail_mask):
    laplace = prev_rows - 2.0 * wave_in + next_rows
    right_re, right_im = times_complex(kappa_re, -kappa_im, laplace[0], laplace[1])
    return pack_system(
        [
            (kappa_re * head_mask, kappa_im * head_mask),
            (-2.0 * kappa_re, -2.0 * kappa_im),
            (kappa_re * tail_mask, kappa_im * tail_mask),
            (wave_in[0] + right_re, wave_in[1] + right_im),
        ]
    )


def reduce_level(system, below, above):
    alpha_re, alpha_im = divide_complex(
        -system[0, 0], -system[0, 1], below[1, 0] + 1.0, below[1, 1]
    )
    gamma_re, gamma_im = divide_complex(
        -system[2, 0], -system[2, 1], above[1, 0] + 1.0, above[1, 1]
    )
    lower_coef = times_complex(alpha_re, alpha_im, below[0, 0], below[0, 1])
    upper_coef = times_complex(gamma_re, gamma_im, above[2, 0], above[2, 1])
    left_diag = times_complex(alpha_re, alpha_im, below[2, 0], below[2, 1])
    right_diag = times_complex(gamma_re, gamma_im, above[0, 0], above[0, 1])
    left_rhs = times_complex(alpha_re, alpha_im, below[3, 0], below[3, 1])
    right_rhs = times_complex(gamma_re, gamma_im, above[3, 0], above[3, 1])
    center = (
        system[1, 0] + left_diag[0] + right_diag[0],
        system[1, 1] + left_diag[1] + right_diag[1],
    )
    source = (system[3, 0] + left_rhs[0] + right_rhs[0], system[3, 1] + left_rhs[1] + right_rhs[1])
    return pack_system([lower_coef, center, upper_coef, source])


def finish(system):
    sol_re, sol_im = divide_complex(system[3, 0], system[3, 1], system[1, 0] + 1.0, system[1, 1])
    return jnp.stack([sol_re, sol_im])


def move_near(piece, offset):
    return shifted(piece, "gx", offset)


def move_far(piece, offset):
    return shifted(piece, "gx", offset)


def remote_below(system, stride, cells_x):
    if stride < cells_x:
        return jnp.concatenate(
            [
                move_near(system[:, :, :, cells_x - stride :], 1),
                system[:, :, :, : cells_x - stride],
            ],
            axis=3,
        )
    return move_far(system, stride // cells_x)


def remote_above(system, stride, cells_x):
    if stride < cells_x:
        return jnp.concatenate(
            [system[:, :, :, stride:], move_near(system[:, :, :, :stride], -1)], axis=3
        )
    return move_far(system, -(stride // cells_x))


def chain_solve(wave_in, kappa_re, kappa_im, cells_x, strips):
    padded = padded_2(wave_in, (("gx", 2),), 1)
    places = (lax.axis_index("gx") * cells_x + jnp.arange(cells_x)).reshape(1, cells_x, 1)
    total_cells = cells_x * strips
    head_mask = (places > 0).astype(jnp.float32)
    tail_mask = (places < total_cells - 1).astype(jnp.float32)
    system = build(
        wave_in, kappa_re, kappa_im, padded[:, :, :-2], padded[:, :, 2:], head_mask, tail_mask
    )
    stride = 1
    while stride < total_cells:
        system = reduce_level(
            system, remote_below(system, stride, cells_x), remote_above(system, stride, cells_x)
        )
        stride = stride * 2
    return finish(system)


def screen(wave_in, velocity, angular):
    angle_now = angular * PHASE * (1.0 / velocity - 1.0 / 3.0)
    new_re, new_im = times_complex(wave_in[0], wave_in[1], jnp.cos(angle_now), jnp.sin(angle_now))
    return jnp.stack([new_re, new_im])


def shards(wavefield, velocity_bank, owner):
    freq_local = wavefield.shape[1]
    cells_x = wavefield.shape[2]
    strips = lax.axis_size("gx")
    freq_total = freq_local * lax.axis_size("freq")
    indices = lax.axis_index("freq") * freq_local + jnp.arange(freq_local)
    angular = (1.0 + 3.0 * indices.astype(jnp.float32) / freq_total).reshape(freq_local, 1, 1)
    wave_now = wavefield
    velocity = broadcast(velocity_bank[0], "freq", owner[0])
    wave_now = screen(wave_now, velocity, angular)
    kappa_im = -GAIN * velocity / angular
    kappa_re = jnp.full_like(kappa_im, BETA)
    wave_now = chain_solve(wave_now, kappa_re, kappa_im, cells_x, strips)
    partial_sum = jnp.sum(wave_now[0], axis=0)
    stacked_image = lax.psum(partial_sum, "freq") * (1.0 / math.sqrt(freq_total))
    return (wave_now, stacked_image)


def solution(mesh):
    return jax.shard_map(
        shards,
        mesh=mesh,
        in_specs=(P(None, "freq", "gx", None), P("freq", "gx", None), P()),
        out_specs=(P(None, "freq", "gx", None), P("gx", None)),
        check_vma=False,
    )
```

profile of v0, /device:TPU:1, one launch (start us, length us, event | category | flops | bytes accessed | tf_op | source)
XLA Modules:
  0.0 909.3 jit_solution(11093796970449378960)
XLA Ops:
  7.9 0.6 select_bitcast_fusion
  8.7 321.6 %all-reduce.4.cloned.1.call-done = f32[128,128]{1,0:T(8,128)} async-done(((f32[128,128]{1,0:T(8,128)}), f32[128,128]{1,0:T(8,128)}) %all-reduce.4.cloned.1.call-update) | async-done | bytes 65552 | tf_op jit(solution)/shard_map/psum | solution.py:34
  330.2 0.9 divide_add_fusion
  331.1 0.6 fusion.7
  331.7 3.1 collective-permute-start
  334.8 1.3 collective-permute-start.1
  336.1 3.0 collective-permute-done.1
  339.7 1.3 collective-permute-start.3
  341.0 4.0 collective-permute-start.2
  345.2 0.6 collective-permute-done.2
  346.6 1.3 collective-permute-start.5
  347.9 4.2 collective-permute-start.4
  352.2 0.2 fusion.264
  352.4 0.6 collective-permute-done.4
  353.8 1.3 collective-permute-start.7
  355.1 4.3 collective-permute-start.6
  359.4 0.2 fusion.263
  359.6 0.8 collective-permute-done.6
  361.2 1.3 collective-permute-start.9
  362.5 5.8 collective-permute-start.8
  368.4 1.2 collective-permute-done.8
  370.3 1.3 collective-permute-start.11
  371.6 6.4 collective-permute-start.10
  378.2 1.8 collective-permute-done.10
  380.7 1.3 collective-permute-start.13
  382.0 6.4 collective-permute-start.12
  388.6 3.1 collective-permute-done.12
  392.4 5.8 collective-permute-start.14
  398.2 1.3 collective-permute-start.15
  399.5 7.4 collective-permute-done.14
  407.0 3.6 collective-permute-done.15
  411.1 1.3 collective-permute-start.17
  412.4 7.1 collective-permute-start.16
  419.5 15.8 %collective-permute-done.17 = f32[4,2,2,128,128]{4,3,2,1,0:T(8,128)S(1)} collective-permute-done((f32[4,2,2,128,128]{4,3,2,1,0:T(8,128)S(1)}, f32[4,2,2,128,128]{4,3,2,1,0:T(8,128)S(1)}, u32[]{:S(2)}, u32[]{:S(2)}) %collective-permute-start.17) | collective-permute-done | bytes 1048608 | tf_op jit(solution)/shard_map/ppermute | solution.py:16
  435.9 1.3 collective-permute-start.19
  437.2 10.2 %collective-permute-start.18 = (f32[4,2,2,128,128]{4,3,2,1,0:T(8,128)S(1)}, f32[4,2,2,128,128]{4,3,2,1,0:T(8,128)S(1)}, u32[]{:S(2)}, u32[]{:S(2)}) collective-permute-start(f32[4,2,2,128,128]{4,3,2,1,0:T(8,128)S(1)} %pad_maximum_fusion.8), channel_id=1, source_target_pairs={{0,2},{1,3},{2,4},{3,5},{4,6},{5,7},{6,8},{7,9},{8,10},{9,11},{10,... | collective-permute-start | bytes 3145736 | tf_op jit(solution)/shard_map/ppermute | solution.py:16
  447.4 18.3 %collective-permute-done.19 = f32[4,2,2,128,128]{4,3,2,1,0:T(8,128)S(1)} collective-permute-done((f32[4,2,2,128,128]{4,3,2,1,0:T(8,128)S(1)}, f32[4,2,2,128,128]{4,3,2,1,0:T(8,128)S(1)}, u32[]{:S(2)}, u32[]{:S(2)}) %collective-permute-start.19) | collective-permute-done | bytes 1048608 | tf_op jit(solution)/shard_map/ppermute | solution.py:16
  465.8 8.3 collective-permute-done.18
  474.6 1.3 collective-permute-start.21
  475.9 16.9 %collective-permute-start.20 = (f32[4,2,2,128,128]{4,3,2,1,0:T(8,128)S(1)}, f32[4,2,2,128,128]{4,3,2,1,0:T(8,128)S(1)}, u32[]{:S(2)}, u32[]{:S(2)}) collective-permute-start(f32[4,2,2,128,128]{4,3,2,1,0:T(8,128)S(1)} %pad_maximum_fusion.9), channel_id=1, source_target_pairs={{0,4},{1,5},{2,6},{3,7},{4,8},{5,9},{6,10},{7,11},{8,12},{9,13},{1... | collective-permute-start | bytes 3145736 | tf_op jit(solution)/shard_map/ppermute | solution.py:16
  492.8 16.1 %collective-permute-done.21 = f32[4,2,2,128,128]{4,3,2,1,0:T(8,128)S(1)} collective-permute-done((f32[4,2,2,128,128]{4,3,2,1,0:T(8,128)S(1)}, f32[4,2,2,128,128]{4,3,2,1,0:T(8,128)S(1)}, u32[]{:S(2)}, u32[]{:S(2)}) %collective-permute-start.21) | collective-permute-done | bytes 1048608 | tf_op jit(solution)/shard_map/ppermute | solution.py:16
  509.6 1.3 collective-permute-start.23
  510.9 8.2 collective-permute-start.22
  519.1 30.7 %collective-permute-done.23 = f32[4,2,2,128,128]{4,3,2,1,0:T(8,128)S(1)} collective-permute-done((f32[4,2,2,128,128]{4,3,2,1,0:T(8,128)S(1)}, f32[4,2,2,128,128]{4,3,2,1,0:T(8,128)S(1)}, u32[]{:S(2)}, u32[]{:S(2)}) %collective-permute-start.23) | collective-permute-done | bytes 1048608 | tf_op jit(solution)/shard_map/ppermute | solution.py:16
  550.2 0.7 fusion.234
  551.0 0.7 pad_maximum_fusion.16
  551.7 349.4 %all-reduce.6.cloned.1.call-done = f32[128,128]{1,0:T(8,128)} async-done(((f32[128,128]{1,0:T(8,128)}), f32[128,128]{1,0:T(8,128)}) %all-reduce.6.cloned.1.call-update) | async-done | bytes 65552 | tf_op jit(solution)/shard_map/psum | solution.py:158
  901.0 1.5 broadcast_multiply_fusion
  (142 shorter events, 8.2 us)
Async XLA Ops:
  7.2 323.9 %copy-start = (f32[2,2,128,128]{3,2,1,0:T(8,128)S(1)}, f32[2,2,128,128]{3,2,1,0:T(8,128)}, u32[]{:S(2)}) copy-start(f32[2,2,128,128]{3,2,1,0:T(8,128)} %param.3) | copy-start | bytes 786436
  7.2 323.1 %all-reduce.4.cloned.1.call-start = ((), (), s32[]{:S(2)}) async-start(), calls=%async_computation | async-start | bytes 131072 | tf_op jit(solution)/shard_map/psum | solution.py:34
  8.6 892.5 %all-reduce.6.cloned.1.call-start = ((), (), s32[]{:S(2)}) async-start(), calls=%async_computation.1 | async-start | bytes 131072 | tf_op jit(solution)/shard_map/psum | solution.py:158
  331.7 4.4 collective-permute-start
  334.8 4.3 collective-permute-start.1
  339.7 6.2 collective-permute-start.3
  341.0 4.8 collective-permute-start.2
  346.6 6.5 collective-permute-start.5
  347.9 5.1 collective-permute-start.4
  353.8 6.7 collective-permute-start.7
  355.1 5.3 collective-permute-start.6
  361.2 8.5 collective-permute-start.9
  362.5 7.1 collective-permute-start.8
  370.3 9.7 %collective-permute-start.11 = (f32[4,2,2,16,128]{4,3,2,1,0:T(8,128)S(1)}, f32[4,2,2,16,128]{4,3,2,1,0:T(8,128)S(1)}, u32[]{:S(2)}, u32[]{:S(2)}) collective-permute-start(f32[4,2,2,16,128]{4,3,2,1,0:T(8,128)S(1)} %get-tuple-element.153), channel_id=1, source_target_pairs={{1,0},{2,1},{3,2},{4,3},{5,4},{6,5},{7,6},{8,7},{9,8},{10,9},{11,1... | collective-permute-start | bytes 393224 | tf_op jit(solution)/shard_map/ppermute | solution.py:16
  371.6 8.3 collective-permute-start.10
  380.7 11.1 %collective-permute-start.13 = (f32[4,2,2,32,128]{4,3,2,1,0:T(8,128)S(1)}, f32[4,2,2,32,128]{4,3,2,1,0:T(8,128)S(1)}, u32[]{:S(2)}, u32[]{:S(2)}) collective-permute-start(f32[4,2,2,32,128]{4,3,2,1,0:T(8,128)S(1)} %get-tuple-element.149), channel_id=1, source_target_pairs={{1,0},{2,1},{3,2},{4,3},{5,4},{6,5},{7,6},{8,7},{9,8},{10,9},{11,1... | collective-permute-start | bytes 786440 | tf_op jit(solution)/shard_map/ppermute | solution.py:16
  382.0 9.7 %collective-permute-start.12 = (f32[4,2,2,32,128]{4,3,2,1,0:T(8,128)S(1)}, f32[4,2,2,32,128]{4,3,2,1,0:T(8,128)S(1)}, u32[]{:S(2)}, u32[]{:S(2)}) collective-permute-start(f32[4,2,2,32,128]{4,3,2,1,0:T(8,128)S(1)} %get-tuple-element.150), channel_id=1, source_target_pairs={{0,1},{1,2},{2,3},{3,4},{4,5},{5,6},{6,7},{7,8},{8,9},{9,10},{10,1... | collective-permute-start | bytes 786440 | tf_op jit(solution)/shard_map/ppermute | solution.py:16
  392.4 14.5 %collective-permute-start.14 = (f32[4,2,2,64,128]{4,3,2,1,0:T(8,128)S(1)}, f32[4,2,2,64,128]{4,3,2,1,0:T(8,128)S(1)}, u32[]{:S(2)}, u32[]{:S(2)}) collective-permute-start(f32[4,2,2,64,128]{4,3,2,1,0:T(8,128)S(1)} %get-tuple-element.145), channel_id=1, source_target_pairs={{0,1},{1,2},{2,3},{3,4},{4,5},{5,6},{6,7},{7,8},{8,9},{9,10},{10,1... | collective-permute-start | bytes 1572872 | tf_op jit(solution)/shard_map/ppermute | solution.py:16
  398.2 12.4 %collective-permute-start.15 = (f32[4,2,2,64,128]{4,3,2,1,0:T(8,128)S(1)}, f32[4,2,2,64,128]{4,3,2,1,0:T(8,128)S(1)}, u32[]{:S(2)}, u32[]{:S(2)}) collective-permute-start(f32[4,2,2,64,128]{4,3,2,1,0:T(8,128)S(1)} %get-tuple-element.146), channel_id=1, source_target_pairs={{1,0},{2,1},{3,2},{4,3},{5,4},{6,5},{7,6},{8,7},{9,8},{10,9},{11,1... | collective-permute-start | bytes 1572872 | tf_op jit(solution)/shard_map/ppermute | solution.py:16
  411.1 24.2 %collective-permute-start.17 = (f32[4,2,2,128,128]{4,3,2,1,0:T(8,128)S(1)}, f32[4,2,2,128,128]{4,3,2,1,0:T(8,128)S(1)}, u32[]{:S(2)}, u32[]{:S(2)}) collective-permute-start(f32[4,2,2,128,128]{4,3,2,1,0:T(8,128)S(1)} %pad_maximum_fusion.7), channel_id=1, source_target_pairs={{1,0},{2,1},{3,2},{4,3},{5,4},{6,5},{7,6},{8,7},{9,8},{10,9},{11,1... | collective-permute-start | bytes 3145736 | tf_op jit(solution)/shard_map/ppermute | solution.py:16
  412.4 23.0 %collective-permute-start.16 = (f32[4,2,2,128,128]{4,3,2,1,0:T(8,128)S(1)}, f32[4,2,2,128,128]{4,3,2,1,0:T(8,128)S(1)}, u32[]{:S(2)}, u32[]{:S(2)}) collective-permute-start(f32[4,2,2,128,128]{4,3,2,1,0:T(8,128)S(1)} %pad_maximum_fusion.7), channel_id=1, source_target_pairs={{0,1},{1,2},{2,3},{3,4},{4,5},{5,6},{6,7},{7,8},{8,9},{9,10},{10,1... | collective-permute-start | bytes 3145736 | tf_op jit(solution)/shard_map/ppermute | solution.py:16
  435.9 29.8 %collective-permute-start.19 = (f32[4,2,2,128,128]{4,3,2,1,0:T(8,128)S(1)}, f32[4,2,2,128,128]{4,3,2,1,0:T(8,128)S(1)}, u32[]{:S(2)}, u32[]{:S(2)}) collective-permute-start(f32[4,2,2,128,128]{4,3,2,1,0:T(8,128)S(1)} %pad_maximum_fusion.8), channel_id=1, source_target_pairs={{2,0},{3,1},{4,2},{5,3},{6,4},{7,5},{8,6},{9,7},{10,8},{11,9},{12,... | collective-permute-start | bytes 3145736 | tf_op jit(solution)/shard_map/ppermute | solution.py:16
  437.2 36.9 %collective-permute-start.18 = (f32[4,2,2,128,128]{4,3,2,1,0:T(8,128)S(1)}, f32[4,2,2,128,128]{4,3,2,1,0:T(8,128)S(1)}, u32[]{:S(2)}, u32[]{:S(2)}) collective-permute-start(f32[4,2,2,128,128]{4,3,2,1,0:T(8,128)S(1)} %pad_maximum_fusion.8), channel_id=1, source_target_pairs={{0,2},{1,3},{2,4},{3,5},{4,6},{5,7},{6,8},{7,9},{8,10},{9,11},{10,... | collective-permute-start | bytes 3145736 | tf_op jit(solution)/shard_map/ppermute | solution.py:16
  474.6 34.3 %collective-permute-start.21 = (f32[4,2,2,128,128]{4,3,2,1,0:T(8,128)S(1)}, f32[4,2,2,128,128]{4,3,2,1,0:T(8,128)S(1)}, u32[]{:S(2)}, u32[]{:S(2)}) collective-permute-start(f32[4,2,2,128,128]{4,3,2,1,0:T(8,128)S(1)} %pad_maximum_fusion.9), channel_id=1, source_target_pairs={{4,0},{5,1},{6,2},{7,3},{8,4},{9,5},{10,6},{11,7},{12,8},{13,9},{1... | collective-permute-start | bytes 3145736 | tf_op jit(solution)/shard_map/ppermute | solution.py:16
  475.9 33.1 %collective-permute-start.20 = (f32[4,2,2,128,128]{4,3,2,1,0:T(8,128)S(1)}, f32[4,2,2,128,128]{4,3,2,1,0:T(8,128)S(1)}, u32[]{:S(2)}, u32[]{:S(2)}) collective-permute-start(f32[4,2,2,128,128]{4,3,2,1,0:T(8,128)S(1)} %pad_maximum_fusion.9), channel_id=1, source_target_pairs={{0,4},{1,5},{2,6},{3,7},{4,8},{5,9},{6,10},{7,11},{8,12},{9,13},{1... | collective-permute-start | bytes 3145736 | tf_op jit(solution)/shard_map/ppermute | solution.py:16
  509.6 40.3 %collective-permute-start.23 = (f32[4,2,2,128,128]{4,3,2,1,0:T(8,128)S(1)}, f32[4,2,2,128,128]{4,3,2,1,0:T(8,128)S(1)}, u32[]{:S(2)}, u32[]{:S(2)}) collective-permute-start(f32[4,2,2,128,128]{4,3,2,1,0:T(8,128)S(1)} %pad_maximum_fusion.10), channel_id=1, source_target_pairs={{8,0},{9,1},{10,2},{11,3},{12,4},{13,5},{14,6},{15,7},{24,16},{25,... | collective-permute-start | bytes 3145736 | tf_op jit(solution)/shard_map/ppermute | solution.py:16
  510.9 39.0 %collective-permute-start.22 = (f32[4,2,2,128,128]{4,3,2,1,0:T(8,128)S(1)}, f32[4,2,2,128,128]{4,3,2,1,0:T(8,128)S(1)}, u32[]{:S(2)}, u32[]{:S(2)}) collective-permute-start(f32[4,2,2,128,128]{4,3,2,1,0:T(8,128)S(1)} %pad_maximum_fusion.10), channel_id=1, source_target_pairs={{0,8},{1,9},{2,10},{3,11},{4,12},{5,13},{6,14},{7,15},{16,24},{17,... | collective-permute-start | bytes 3145736 | tf_op jit(solution)/shard_map/ppermute | solution.py:16
Sparse Core Ops, SparseCore 0:
  11.5 318.6 all-reduce.3
  551.1 349.9 all-reduce.5
where the time goes:
time: 911 us; the launch traced here: 909 us
  waiting for transfers between devices  782 us (86%)
  starting transfers between devices  97.9 us (11%)
  between operations  15.8 us (2%)
  other arithmetic  12 us (1%)
    psum x1, waiting for transfers between devices, shards(): lax.psum(partial_sum, 'freq') * (1.0 / math.sqrt(freq_total))  349 us
    psum x1, waiting for transfers between devices, broadcast(): return lax.psum(kept, axis)  322 us
    ppermute x22, waiting for transfers between devices, shifted(): return lax.ppermute(block, axis, route)  108 us
    ppermute x22, starting transfers between devices, shifted(): return lax.ppermute(block, axis, route)  93.4 us
  transfers between devices with their start and end apart: 26, of which 16 were waited for; matrix products, arithmetic and copies ran while one was open for 0% of the time, Pallas kernels for 0%

commit v1 on v0

v1 whole, which is shorter than its diff:
```python
import functools
import math

import jax
import jax.numpy as jnp
from jax import lax
from jax.experimental import pallas as pl
from jax.experimental.pallas import tpu as pltpu
from jax.sharding import Mesh, PartitionSpec as P

BETA = 1.0 / 6.0
GAIN = 30000.0
PHASE = 2.0

ZH, YY, CC, ZL, XX = 4, 4, 2, 4, 4
FREQ = ("zh", "y", "c")
STRIPS = ("zl", "x")
N_STRIPS = ZL * XX
SEGMENTS = 8
FIELDS = 7
MESSAGE = 32


def mul(a, b):
    return (a[0] * b[0] - a[1] * b[1], a[0] * b[1] + a[1] * b[0])


def add(a, b):
    return (a[0] + b[0], a[1] + b[1])


def sub(a, b):
    return (a[0] - b[0], a[1] - b[1])


def neg(a):
    return (-a[0], -a[1])


def scale(s, a):
    return (s * a[0], s * a[1])


def reciprocal(a):
    inverse = 1.0 / (a[0] * a[0] + a[1] * a[1])
    return (a[0] * inverse, -a[1] * inverse)


def sin_cos(angle):
    h = 0.5 * angle
    z = h * h
    s = 1.0 / 6227020800.0
    for k in (-1.0 / 39916800.0, 1.0 / 362880.0, -1.0 / 5040.0, 1.0 / 120.0, -1.0 / 6.0):
        s = s * z + k
    s = h + h * (z * s)
    c = 1.0 / 87178291200.0
    c = -c * z + 1.0 / 479001600.0
    for k in (-1.0 / 3628800.0, 1.0 / 40320.0, -1.0 / 720.0, 1.0 / 24.0, -0.5):
        c = c * z + k
    c = 1.0 + z * c
    return 2.0 * s * c, 1.0 - 2.0 * s * s


def inverse_kappa(velocity, angular):
    big = GAIN * velocity * (1.0 / angular)
    inverse = 1.0 / (BETA * BETA + big * big)
    return (BETA * inverse, big * inverse)


def angular_of(f, freq_local, freq_total):
    index = (lax.axis_index("zh") * YY + lax.axis_index("y")) * CC + lax.axis_index("c")
    index = index * freq_local + f
    return 1.0 + 3.0 * index.astype(jnp.float32) / freq_total


def shift_rows(x, distance, rows):
    count = x.shape[0]
    rolled = pltpu.roll(x, distance % count, 0)
    inside = rows >= distance if distance > 0 else rows < count + distance
    return jnp.where(inside, rolled, 0.0)


def shift_pair(a, distance, rows):
    return (shift_rows(a[0], distance, rows), shift_rows(a[1], distance, rows))


def source_terms(wave, t, steps, eps, rows):
    here = wave(t)
    prev = wave(t - 1) if t > 0 else shift_pair(wave(steps - 1), 1, rows)
    after = wave(t + 1) if t < steps - 1 else shift_pair(wave(0), -1, rows)
    lap = sub(add(prev, after), scale(2.0, here))
    return mul(scale(2.0, eps), add(here, scale(BETA, lap)))


def forward_kernel(freq_total, owner_ref, wave_ref, vel_ref, screened_ref, scan_ref, message_ref, rows_ref):
    freq_local, cells = wave_ref.shape[1], wave_ref.shape[2]
    steps = cells // SEGMENTS
    lanes = wave_ref.shape[3]
    core = lax.rem(owner_ref[0], CC)
    rows = lax.broadcasted_iota(jnp.int32, (SEGMENTS, lanes), 0)
    one = jnp.ones((SEGMENTS, lanes), jnp.float32)
    zero = jnp.zeros((SEGMENTS, lanes), jnp.float32)
    omegas = [angular_of(f, freq_local, freq_total) for f in range(freq_local)]

    def velocity(t):
        return vel_ref[core, pl.ds(t, SEGMENTS, stride=steps), :]

    for t in range(steps):
        psi = PHASE * (1.0 / velocity(t) - 1.0 / 3.0)
        for f in range(freq_local):
            sin, cos = sin_cos(omegas[f] * psi)
            re = wave_ref[0, f, pl.ds(t, SEGMENTS, stride=steps), :]
            im = wave_ref[1, f, pl.ds(t, SEGMENTS, stride=steps), :]
            screened_ref[f, 0, t] = re * cos - im * sin
            screened_ref[f, 1, t] = re * sin + im * cos

    rows_ref[...] = jnp.zeros(rows_ref.shape, jnp.float32)
    for f in range(freq_local):
        wave = lambda t: (screened_ref[f, 0, t], screened_ref[f, 1, t])
        state = [[(one, zero), (zero, zero)], [(zero, zero), (one, zero)], [(zero, zero), (zero, zero)]]
        for t in range(steps):
            eps = inverse_kappa(velocity(t), omegas[f])
            g = source_terms(wave, t, steps, eps, rows)
            for i in range(3):
                w, d = state[i]
                d = sub(d, mul(eps, w))
                if i == 2:
                    d = add(d, g)
                state[i] = [add(w, d), d]
        (m00, m10), (m01, m11), (v0, v1) = state
        distance = 1
        while distance < SEGMENTS:
            b00, b01, b10, b11, bv0, bv1 = [
                (pltpu.roll(q[0], distance, 0), pltpu.roll(q[1], distance, 0))
                for q in (m00, m01, m10, m11, v0, v1)
            ]
            new = (
                add(mul(m00, b00), mul(m01, b10)),
                add(mul(m00, b01), mul(m01, b11)),
                add(mul(m10, b00), mul(m11, b10)),
                add(mul(m10, b01), mul(m11, b11)),
                add(add(mul(m00, bv0), mul(m01, bv1)), v0),
                add(add(mul(m10, bv0), mul(m11, bv1)), v1),
            )
            use = rows >= distance
            m00, m01, m10, m11, v0, v1 = [
                (jnp.where(use, n[0], q[0]), jnp.where(use, n[1], q[1]))
                for n, q in zip(new, (m00, m01, m10, m11, v0, v1))
            ]
            distance *= 2
        for i, q in enumerate((m00, m01, m10, m11, v0, v1)):
            scan_ref[f, 2 * i] = q[0]
            scan_ref[f, 2 * i + 1] = q[1]
        r = reciprocal(m01)
        b = mul(m11, r)
        fields = (r, mul(m00, r), b, mul(r, v0), sub(v1, mul(b, v0)))
        base = f * FIELDS * 2
        for i, q in enumerate(fields):
            for c in range(2):
                rows_ref[base + 2 * i + c : base + 2 * i + c + 1, :] = q[c][SEGMENTS - 1 :, :]
        for c in range(2):
            rows_ref[base + 10 + c : base + 11 + c, :] = screened_ref[f, c, 0][0:1, :]
            rows_ref[base + 12 + c : base + 13 + c, :] = screened_ref[f, c, steps - 1][SEGMENTS - 1 :, :]
    tail = freq_local * FIELDS * 2
    rows_ref[tail : tail + 1, :] = velocity(0)[0:1, :]
    rows_ref[tail + 1 : tail + 2, :] = velocity(steps - 1)[SEGMENTS - 1 :, :]
    whole = rows_ref[...]
    for s in range(message_ref.shape[0]):
        message_ref[s] = whole


def backward_kernel(freq_total, owner_ref, gathered_ref, screened_ref, scan_ref, vel_ref, out_ref, image_ref, pick_ref):
    freq_local, cells = out_ref.shape[1], out_ref.shape[2]
    steps = cells // SEGMENTS
    lanes = out_ref.shape[3]
    strips = gathered_ref.shape[0] // MESSAGE
    core = lax.rem(owner_ref[0], CC)
    strip = lax.axis_index("zl") * XX + lax.axis_index("x")
    rows = lax.broadcasted_iota(jnp.int32, (SEGMENTS, lanes), 0)
    places = lax.broadcasted_iota(jnp.int32, (strips, lanes), 0)
    omegas = [angular_of(f, freq_local, freq_total) for f in range(freq_local)]

    def field(i):
        return gathered_ref[pl.ds(i, strips, stride=MESSAGE), :]

    tail = freq_local * FIELDS * 2
    vel_head, vel_tail = field(tail), field(tail + 1)
    for f in range(freq_local):
        base = f * FIELDS * 2
        r, a, b, q0, q1, p_head, p_tail = [
            (field(base + 2 * i), field(base + 2 * i + 1)) for i in range(FIELDS)
        ]
        eps_head = inverse_kappa(vel_head, omegas[f])
        eps_tail = inverse_kappa(vel_tail, omegas[f])
        e = mul(scale(2.0 * BETA, eps_head), shift_pair(p_tail, 1, places))
        c = mul(scale(2.0 * BETA, eps_tail), shift_pair(p_head, -1, places))
        carry = add(q1, sub(c, mul(c, b)))
        inner = add(q0, mul(r, c))
        rhs = add(add(inner, e), shift_pair(carry, 1, places))
        b_below = shift_pair(b, 1, places)
        diag = add(a, (jnp.where(places == 0, 1.0, b_below[0]), b_below[1]))
        inv = neg(reciprocal(diag))
        low = mul(shift_pair(r, 1, places), inv)
        edge = places == strips - 1
        up = mul((jnp.where(edge, 0.0, r[0]), jnp.where(edge, 0.0, r[1])), inv)
        rhs = mul(rhs, inv)
        distance = 1
        while distance < strips:
            low_b, up_b, rhs_b = [shift_pair(q, distance, places) for q in (low, up, rhs)]
            low_a, up_a, rhs_a = [shift_pair(q, -distance, places) for q in (low, up, rhs)]
            pivot = add(mul(low, up_b), mul(up, low_a))
            inv = reciprocal((1.0 - pivot[0], -pivot[1]))
            rhs = mul(sub(rhs, add(mul(low, rhs_b), mul(up, rhs_a))), inv)
            if 2 * distance < strips:
                low, up = neg(mul(mul(low, low_b), inv)), neg(mul(mul(up, up_a), inv))
            distance *= 2
        slope = sub(mul(r, shift_pair(rhs, -1, places)), add(mul(a, rhs), inner))
        for i, q in enumerate((rhs[0], rhs[1], slope[0], slope[1])):
            pick_ref[4 * f + i] = q

    state = []
    for f in range(freq_local):
        w_in, d_in = [
            tuple(
                jnp.broadcast_to(pick_ref[4 * f + 2 * i + c, pl.ds(strip, 1), :], (SEGMENTS, lanes))
                for c in range(2)
            )
            for i in range(2)
        ]
        m00, m01, m10, m11, v0, v1 = [
            shift_pair((scan_ref[f, 2 * i], scan_ref[f, 2 * i + 1]), 1, rows) for i in range(6)
        ]
        first = rows == 0
        m00 = (jnp.where(first, 1.0, m00[0]), m00[1])
        m11 = (jnp.where(first, 1.0, m11[0]), m11[1])
        w = add(add(mul(m00, w_in), mul(m01, d_in)), v0)
        d = add(add(mul(m10, w_in), mul(m11, d_in)), v1)
        state.append((w, d))
    for t in range(steps):
        image = None
        vel = vel_ref[core, pl.ds(t, SEGMENTS, stride=steps), :]
        for f in range(freq_local):
            wave = lambda t: (screened_ref[f, 0, t], screened_ref[f, 1, t])
            w, d = state[f]
            out = sub(w, wave(t))
            out_ref[0, f, pl.ds(t, SEGMENTS, stride=steps), :] = out[0]
            out_ref[1, f, pl.ds(t, SEGMENTS, stride=steps), :] = out[1]
            image = out[0] if image is None else image + out[0]
            if t < steps - 1:
                eps = inverse_kappa(vel, omegas[f])
                d = add(sub(d, mul(eps, w)), source_terms(wave, t, steps, eps, rows))
                state[f] = (add(w, d), d)
        image_ref[pl.ds(t, SEGMENTS, stride=steps), :] = image


def tree(axes, index, count, source, value):
    place, core = source

    def pair(a, b):
        return ((a % count) * CC + core, (b % count) * CC + core)

    up = lax.ppermute(value, axes, [pair(place, place + 1)])
    far = lax.ppermute(up, axes, [pair(place + 1, place + 2)])
    down = lax.ppermute(value, axes, [pair(place, place - 1)])
    return jnp.where(index == place, value, up + far + down)


def spread(value, axis, count, place, core):
    index = lax.axis_index(axis)
    branches = [
        functools.partial(tree, (axis, "c"), index, count, (p, c)) for p in range(count) for c in range(CC)
    ]
    return lax.switch(place * CC + core, branches, value)


def strip_call(kernel, outs, scratch, smem_args, args):
    return pl.pallas_call(
        kernel,
        out_shape=outs,
        in_specs=[pl.BlockSpec(memory_space=pltpu.SMEM)] * smem_args
        + [pl.BlockSpec(memory_space=pltpu.VMEM)] * (len(args) - smem_args),
        out_specs=[pl.BlockSpec(memory_space=pltpu.VMEM)] * len(outs),
        scratch_shapes=scratch,
        compiler_params=pltpu.CompilerParams(vmem_limit_bytes=32 * 1024 * 1024),
    )(*args)


PAIRS_ONE = [(0, 1), (1, 0), (2, 3), (3, 2)]
PAIRS_TWO = [(1, 2), (2, 1), (3, 0), (0, 3)]


def shards(wavefield, velocity_bank, owner):
    freq_local, cells, lanes = wavefield.shape[1:]
    steps = cells // SEGMENTS
    freq_total = freq_local * ZH * YY * CC
    struct = lambda *shape: jax.ShapeDtypeStruct(shape, jnp.float32)
    own = owner[0]
    core = own % CC
    velocity = spread(velocity_bank[0], "zh", ZH, own // (YY * CC), core)
    velocity = spread(velocity, "y", YY, (own // CC) % YY, core)
    velocity = lax.all_gather(velocity, "c", axis=0)
    screened, scan, message = strip_call(
        functools.partial(forward_kernel, freq_total),
        [
            struct(freq_local, 2, steps, SEGMENTS, lanes),
            struct(freq_local, 12, SEGMENTS, lanes),
            struct(N_STRIPS, MESSAGE, lanes),
        ],
        [pltpu.VMEM((MESSAGE, lanes), jnp.float32)],
        1,
        (owner, wavefield, velocity),
    )
    gathered = lax.all_to_all(message, STRIPS, 0, 0, tiled=True)
    wave_out, partial = strip_call(
        functools.partial(backward_kernel, freq_total),
        [struct(2, freq_local, cells, lanes), struct(cells, lanes)],
        [pltpu.VMEM((4 * freq_local, N_STRIPS, lanes), jnp.float32)],
        1,
        (owner, gathered.reshape(N_STRIPS * MESSAGE, lanes), screened, scan, velocity),
    )
    group = YY * CC
    pieces = lax.all_to_all(partial.reshape(group, cells // group, lanes), ("y", "c"), 0, 0, tiled=True)
    total = jnp.sum(pieces, axis=0)
    total = total + lax.ppermute(total, "zh", PAIRS_ONE)
    total = total + lax.ppermute(total, "zh", PAIRS_TWO)
    total = total * (1.0 / math.sqrt(freq_total))
    image = lax.all_to_all(
        jnp.broadcast_to(total, (group,) + total.shape), ("y", "c"), 0, 0, tiled=True
    )
    return (wave_out, image.reshape(cells, lanes))


def solution(mesh):
    grid = Mesh(mesh.devices.reshape(ZH, YY, CC, ZL, XX), FREQ + STRIPS)
    return jax.shard_map(
        shards,
        mesh=grid,
        in_specs=(P(None, FREQ, STRIPS, None), P(FREQ, STRIPS, None), P()),
        out_specs=(P(None, FREQ, STRIPS, None), P(STRIPS, None)),
        check_vma=False,
    )
```

time: 911 us -> 108 us (0.12)
  waiting for transfers between devices: 782 us -> 15.8 us
  starting transfers between devices: 97.9 us -> 21.7 us
  blocking collectives: 0 us -> 65.5 us
  between operations: 15.8 us -> 1.43 us
  other arithmetic: 12 us -> 0.05 us
    psum x2 -> x0, waiting for transfers between devices: 671 us -> none  [the longest x1 349 us: shards(): lax.psum(partial_sum, 'freq') * (1.0 / math.sqrt(freq_total))]
    ppermute x24 -> x8, waiting for transfers between devices: 111 us -> 15.8 us  [the longest x1 9.39 us: shards(): total = total + lax.ppermute(total, 'zh', PAIRS_TWO)]
    ppermute x24 -> x8, starting transfers between devices: 97.8 us -> 21.7 us  [the longest x1 15.7 us: shards(): total = total + lax.ppermute(total, 'zh', PAIRS_TWO)]
    all_to_all x0 -> x3, blocking collectives: none -> 34.1 us  [the longest x1 13.9 us: shards(): gathered = lax.all_to_all(message, STRIPS, 0, 0, tiled=True)]
    all_gather x0 -> x1, blocking collectives: none -> 31.4 us  [shards(): velocity = lax.all_gather(velocity, 'c', axis=0)]
  transfers between devices with their start and end apart: 26 -> 8, of which waited for: 16 -> 2; matrix products, arithmetic and copies ran while one was open for 0% -> 0% of each run, Pallas kernels for 0% -> 0%
where the time goes in v1:
time: 108 us; the launch traced here: 107 us
  blocking collectives  65.5 us (61%)
  starting transfers between devices  21.7 us (20%)
  waiting for transfers between devices  15.8 us (15%)
  Pallas kernels  1.97 us (2%)
  between operations  1.43 us (1%)
    all_gather x1, blocking collectives, shards(): velocity = lax.all_gather(velocity, 'c', axis=0)  31.4 us
    ppermute x1, starting transfers between devices, shards(): total = total + lax.ppermute(total, 'zh', PAIRS_TWO)  15.7 us
    all_to_all x1, blocking collectives, shards(): gathered = lax.all_to_all(message, STRIPS, 0, 0, tiled=True)  13.9 us
    all_to_all x1, blocking collectives, shards(): lax.all_to_all(jnp.broadcast_to(total, (group,) + total.shape), ('y', 'c'...  10.2 us
    all_to_all x1, blocking collectives, shards(): lax.all_to_all(partial.reshape(group, cells // group, lanes), ('y', 'c'),...  9.97 us
    ppermute x1, waiting for transfers between devices, shards(): total = total + lax.ppermute(total, 'zh', PAIRS_TWO)  9.39 us
    ppermute x1, waiting for transfers between devices, shards(): total = total + lax.ppermute(total, 'zh', PAIRS_ONE)  6.39 us
  transfers between devices with their start and end apart: 8, of which 2 were waited for; matrix products, arithmetic and copies ran while one was open for 0% of the time, Pallas kernels for 0%

profile of v1, /device:TPU:1, one launch (start us, length us, event | category | flops | bytes accessed | tf_op | source)
XLA Modules:
  0.0 107.3 jit_solution(9979938401406509189)
XLA Ops:
  0.6 0.0 copy-start.1
  1.4 0.1 copy-done.1
  1.5 2.1 %conditional.2 = (f32[128,128]{1,0:T(8,128)S(1)}) conditional(s32[]{:T(128)} %clamp.7, (s32[]{:T(128)}, f32[128,128]{1,0:T(8,128)S(1)}) %tuple.77, (s32[]{:T(128)}, f32[128,128]{1,0:T(8,128)S(1)}) %tuple.78, (s32[]{:T(128)}, f32[128,128]{1,0:T(8,128)S(1)}) %tuple.79, (s32[]{:T(128)}, ...), branch_computations={%region_0.1_spmd, %region_1.2_spmd, %region_2.3_spmd, %region_3.4_... | conditional | flops 49153 | bytes 1114250 | solution.py:273
  1.5 0.7 collective-permute-start.6
  2.1 0.7 collective-permute-start.8
  2.8 0.0 collective-permute-done.6
  2.8 0.7 collective-permute-start.7
  3.5 0.0 collective-permute-done.8
  3.5 0.0 collective-permute-done.7
  3.6 0.0 copy-start
  3.6 2.3 %conditional.3 = (f32[128,128]{1,0:T(8,128)S(1)}) conditional(s32[]{:T(128)} %clamp.6, (s32[]{:T(128)}, f32[128,128]{1,0:T(8,128)S(1)}) %tuple.57, (s32[]{:T(128)}, f32[128,128]{1,0:T(8,128)S(1)}) %tuple.57, (s32[]{:T(128)}, f32[128,128]{1,0:T(8,128)S(1)}) %tuple.57, (s32[]{:T(128)}, ...), branch_computations={%region_8.9_spmd, %region_9.10_spmd, %region_10.11_spmd, %region_1... | conditional | flops 49153 | bytes 1114250 | solution.py:273
  3.6 0.8 collective-permute-start.42
  4.4 0.7 collective-permute-start.44
  5.1 0.0 collective-permute-done.42
  5.1 0.7 collective-permute-start.43
  5.8 0.0 collective-permute-done.44
  5.8 0.0 collective-permute-done.43
  5.8 31.4 %all-gather = f32[256,128]{1,0:T(8,128)S(1)} all-gather(f32[128,128]{1,0:T(8,128)S(1)} %get-tuple-element.131), channel_id=2, replica_groups=mesh['zh'=4,'y'=4,'c'=2,'zl'=4,'x'=4] {'c'}, dimensions={0}, use_global_device_ids=true | all-gather | bytes 196608 | tf_op jit(solution)/shard_map/all_gather | solution.py:301
  37.2 0.0 copy-done
  37.2 0.6 shard_map.50
  37.9 13.9 %all_to_all.15 = f32[16,32,128]{2,1,0:T(8,128)S(1)} all-to-all(f32[16,32,128]{2,1,0:T(8,128)S(1)} %get-tuple-element.121), channel_id=1, replica_groups=mesh['zh'=4,'y'=4,'c'=2,'zl'=4,'x'=4] {'zl','x'}, dimensions={0} | all-to-all | bytes 524288 | tf_op jit(solution)/shard_map/all_to_all | solution.py:313
  51.7 1.3 %shard_map.51 = (f32[2,2,128,128]{3,2,1,0:T(8,128)}, f32[128,128]{1,0:T(8,128)S(1)}) custom-call(s32[1]{0:T(128)} %copy.22.owner_ref, f32[512,128]{1,0:T(8,128)S(1)} %bitcast.12, f32[2,2,16,8,128]{4,3,2,1,0:T(8,128)S(1)} %get-tuple-element.122.screened_ref, f32[2,12,8,128]{3,2,1,0:T(8,128)S(1)} %get-tuple-element.123.scan_ref, f32[2,128,128]{2,1,0:T(8,128)S(1)} %bitcast.11), custom_call_target="tpu_custom_call" | custom-call | tf_op jit(solution)/shard_map/pallas_call | solution.py:277
  53.1 10.0 %all_to_all.16 = f32[8,16,128]{2,1,0:T(8,128)S(1)} all-to-all(f32[8,16,128]{2,1,0:T(8,128)S(1)} %bitcast.13), channel_id=1, replica_groups=mesh['zh'=4,'y'=4,'c'=2,'zl'=4,'x'=4] {'y','c'}, dimensions={0} | all-to-all | bytes 131072 | tf_op jit(solution)/shard_map/all_to_all | solution.py:322
  63.0 1.9 %collective-permute-start.48 = (f32[16,128]{1,0:T(8,128)S(1)}, f32[16,128]{1,0:T(8,128)S(1)}, u32[]{:S(2)}, u32[]{:S(2)}) collective-permute-start(f32[16,128]{1,0:T(8,128)S(1)} %reduce_sum.9), channel_id=1, source_target_pairs={{0,128},{128,0},{256,384},{384,256},{1,129},{129,1},{257,385},{385... | collective-permute-start | bytes 24584 | tf_op jit(solution)/shard_map/ppermute | solution.py:324
  65.0 6.4 %collective-permute-done.48 = f32[16,128]{1,0:T(8,128)S(1)} collective-permute-done((f32[16,128]{1,0:T(8,128)S(1)}, f32[16,128]{1,0:T(8,128)S(1)}, u32[]{:S(2)}, u32[]{:S(2)}) %collective-permute-start.48) | collective-permute-done | bytes 8224 | tf_op jit(solution)/shard_map/ppermute | solution.py:324
  71.4 15.7 %collective-permute-start.49 = (f32[16,128]{1,0:T(8,128)S(1)}, f32[16,128]{1,0:T(8,128)S(1)}, u32[]{:S(2)}, u32[]{:S(2)}) collective-permute-start(f32[16,128]{1,0:T(8,128)S(1)} %add.121), channel_id=1, source_target_pairs={{128,256},{256,128},{384,0},{0,384},{129,257},{257,129},{385,1},{1... | collective-permute-start | bytes 24584 | tf_op jit(solution)/shard_map/ppermute | solution.py:325
  87.0 9.4 %collective-permute-done.49 = f32[16,128]{1,0:T(8,128)S(1)} collective-permute-done((f32[16,128]{1,0:T(8,128)S(1)}, f32[16,128]{1,0:T(8,128)S(1)}, u32[]{:S(2)}, u32[]{:S(2)}) %collective-permute-start.49) | collective-permute-done | bytes 8224 | tf_op jit(solution)/shard_map/ppermute | solution.py:325
  96.5 10.2 %all_to_all.17 = f32[8,16,128]{2,1,0:T(8,128)S(1)} all-to-all(f32[8,16,128]{2,1,0:T(8,128)S(1)} %broadcast_in_dim.3), channel_id=1, replica_groups=mesh['zh'=4,'y'=4,'c'=2,'zl'=4,'x'=4] {'y','c'}, dimensions={0} | all-to-all | bytes 131072 | tf_op jit(solution)/shard_map/all_to_all | solution.py:327
  106.7 0.6 copy.23
  (6 shorter events, 0.1 us)
Async XLA Ops:
  0.6 0.8 copy-start.1
  1.5 1.3 %collective-permute-start.6 = (f32[128,128]{1,0:T(8,128)S(1)}, f32[128,128]{1,0:T(8,128)S(1)}, u32[]{:S(2)}, u32[]{:S(2)}) collective-permute-start(f32[128,128]{1,0:T(8,128)S(1)} %get-tuple-element.78), channel_id=1, source_target_pairs={{128,256},{129,257},{130,258},{131,259},{132,260},{133,261},{134,2... | collective-permute-start | bytes 196616 | tf_op jit(solution)/shard_map/cond/branch_2_fun/ppermute | solution.py:262
  2.1 1.4 %collective-permute-start.8 = (f32[128,128]{1,0:T(8,128)S(1)}, f32[128,128]{1,0:T(8,128)S(1)}, u32[]{:S(2)}, u32[]{:S(2)}) collective-permute-start(f32[128,128]{1,0:T(8,128)S(1)} %get-tuple-element.78), channel_id=1, source_target_pairs={{128,0},{129,1},{130,2},{131,3},{132,4},{133,5},{134,6},{135,7},{1... | collective-permute-start | bytes 196616 | tf_op jit(solution)/shard_map/cond/branch_2_fun/ppermute | solution.py:264
  2.8 0.7 collective-permute-start.7
  3.6 33.7 %copy-start = (f32[2,2,128,128]{3,2,1,0:T(8,128)S(1)}, f32[2,2,128,128]{3,2,1,0:T(8,128)}, u32[]{:S(2)}) copy-start(f32[2,2,128,128]{3,2,1,0:T(8,128)} %wave_ref.1) | copy-start | bytes 786436
  3.6 1.5 %collective-permute-start.42 = (f32[128,128]{1,0:T(8,128)S(1)}, f32[128,128]{1,0:T(8,128)S(1)}, u32[]{:S(2)}, u32[]{:S(2)}) collective-permute-start(f32[128,128]{1,0:T(8,128)S(1)} %get-tuple-element.111), channel_id=1, source_target_pairs={{96,0},{97,1},{98,2},{99,3},{100,4},{101,5},{102,6},{103,7},{104,8... | collective-permute-start | bytes 196616 | tf_op jit(solution)/shard_map/cond/branch_6_fun/ppermute | solution.py:262
  4.4 1.4 %collective-permute-start.44 = (f32[128,128]{1,0:T(8,128)S(1)}, f32[128,128]{1,0:T(8,128)S(1)}, u32[]{:S(2)}, u32[]{:S(2)}) collective-permute-start(f32[128,128]{1,0:T(8,128)S(1)} %get-tuple-element.111), channel_id=1, source_target_pairs={{96,64},{97,65},{98,66},{99,67},{100,68},{101,69},{102,70},{103,71... | collective-permute-start | bytes 196616 | tf_op jit(solution)/shard_map/cond/branch_6_fun/ppermute | solution.py:264
  5.1 0.7 collective-permute-start.43
  63.0 8.3 %collective-permute-start.48 = (f32[16,128]{1,0:T(8,128)S(1)}, f32[16,128]{1,0:T(8,128)S(1)}, u32[]{:S(2)}, u32[]{:S(2)}) collective-permute-start(f32[16,128]{1,0:T(8,128)S(1)} %reduce_sum.9), channel_id=1, source_target_pairs={{0,128},{128,0},{256,384},{384,256},{1,129},{129,1},{257,385},{385... | collective-permute-start | bytes 24584 | tf_op jit(solution)/shard_map/ppermute | solution.py:324
  71.4 25.1 %collective-permute-start.49 = (f32[16,128]{1,0:T(8,128)S(1)}, f32[16,128]{1,0:T(8,128)S(1)}, u32[]{:S(2)}, u32[]{:S(2)}) collective-permute-start(f32[16,128]{1,0:T(8,128)S(1)} %add.121), channel_id=1, source_target_pairs={{128,256},{256,128},{384,0},{0,384},{129,257},{257,129},{385,1},{1... | collective-permute-start | bytes 24584 | tf_op jit(solution)/shard_map/ppermute | solution.py:325

commit v2 on v1

--- a/solution.py
+++ b/solution.py
@@ -96,7 +96,7 @@
     freq_local, cells = wave_ref.shape[1], wave_ref.shape[2]
     steps = cells // SEGMENTS
     lanes = wave_ref.shape[3]
-    core = lax.rem(owner_ref[0], CC)
+    core = 0
     rows = lax.broadcasted_iota(jnp.int32, (SEGMENTS, lanes), 0)
     one = jnp.ones((SEGMENTS, lanes), jnp.float32)
     zero = jnp.zeros((SEGMENTS, lanes), jnp.float32)
@@ -174,7 +174,7 @@
     steps = cells // SEGMENTS
     lanes = out_ref.shape[3]
     strips = gathered_ref.shape[0] // MESSAGE
-    core = lax.rem(owner_ref[0], CC)
+    core = 0
     strip = lax.axis_index("zl") * XX + lax.axis_index("x")
     rows = lax.broadcasted_iota(jnp.int32, (SEGMENTS, lanes), 0)
     places = lax.broadcasted_iota(jnp.int32, (strips, lanes), 0)
@@ -273,6 +273,22 @@
     return lax.switch(place * CC + core, branches, value)
 
 
+def spread_plain(value, axis, count, place):
+    index = lax.axis_index(axis)
+
+    def branch(p):
+        def run(x):
+            at = lambda i: i % count
+            far = lax.ppermute(x, axis, [(p, at(p + 2))])
+            up = lax.ppermute(x, axis, [(p, at(p + 1))])
+            down = lax.ppermute(x, axis, [(p, at(p - 1))])
+            return jnp.where(index == p, x, up + far + down)
+
+        return run
+
+    return lax.switch(place, [branch(p) for p in range(count)], value)
+
+
 def strip_call(kernel, outs, scratch, smem_args, args):
     return pl.pallas_call(
         kernel,
@@ -296,9 +312,20 @@
     struct = lambda *shape: jax.ShapeDtypeStruct(shape, jnp.float32)
     own = owner[0]
     core = own % CC
-    velocity = spread(velocity_bank[0], "zh", ZH, own // (YY * CC), core)
-    velocity = spread(velocity, "y", YY, (own // CC) % YY, core)
-    velocity = lax.all_gather(velocity, "c", axis=0)
+    group, rows = YY * CC, cells // (YY * CC)
+    home = own // group
+
+    def scatter(slab):
+        parts = lax.all_to_all(slab.reshape(group, rows, lanes), ("y", "c"), 0, 0, tiled=True)
+        return lax.dynamic_index_in_dim(parts, own % group, 0, keepdims=False)
+
+    piece = lax.cond(
+        lax.axis_index("zh") == home, scatter, lambda slab: slab[:rows], velocity_bank[0]
+    )
+    piece = spread_plain(piece, "zh", ZH, own // group)
+    velocity = lax.all_to_all(
+        jnp.broadcast_to(piece, (group,) + piece.shape), ("y", "c"), 0, 0, tiled=True
+    ).reshape(1, cells, lanes)
     screened, scan, message = strip_call(
         functools.partial(forward_kernel, freq_total),
         [

time: 108 us -> 86.3 us (0.80)
  blocking collectives: 65.5 us -> 44.8 us
  waiting for transfers between devices: 15.8 us -> 7.37 us
  starting transfers between devices: 21.7 us -> 27.7 us
  loops' own time: 0.17 us -> 2.02 us
    all_gather x1 -> x0, blocking collectives: 31.4 us -> none  [shards(): velocity = lax.all_gather(velocity, 'c', axis=0)]
    all_to_all x0 -> x1, blocking collectives: none -> 10.6 us  [shards(): lax.all_to_all(jnp.broadcast_to(piece, (group,) + piece.shape), ('y', 'c'...]
    all_to_all x0 -> x1, starting transfers between devices: none -> 10.3 us  [scatter(): lax.all_to_all(slab.reshape(group, rows, lanes), ('y', 'c'), 0, 0, tiled=...]
    ppermute x1, starting transfers between devices: 15.7 us -> 5.62 us  [shards(): total = total + lax.ppermute(total, 'zh', PAIRS_TWO)]
    ppermute x1, waiting for transfers between devices: 9.39 us -> 2.67 us  [shards(): total = total + lax.ppermute(total, 'zh', PAIRS_TWO)]
    ppermute x1, starting transfers between devices: 1.92 us -> 7.91 us  [shards(): total = total + lax.ppermute(total, 'zh', PAIRS_ONE)]
    ppermute x1, waiting for transfers between devices: 6.39 us -> 1.04 us  [shards(): total = total + lax.ppermute(total, 'zh', PAIRS_ONE)]
    all_to_all x0 -> x1, waiting for transfers between devices: none -> 2.91 us  [scatter(): lax.all_to_all(slab.reshape(group, rows, lanes), ('y', 'c'), 0, 0, tiled=...]
  transfers between devices with their start and end apart: 8 -> 6, of which waited for: 2 -> 4; matrix products, arithmetic and copies ran while one was open for 0% -> 0% of each run, Pallas kernels for 0% -> 0%
where the time goes in v2:
time: 86.3 us; the launch traced here: 85.8 us
  blocking collectives  44.8 us (52%)
  starting transfers between devices  27.7 us (32%)
  waiting for transfers between devices  7.37 us (9%)
  loops' own time  2.02 us (2%)
  Pallas kernels  1.98 us (2%)
  between operations  1.35 us (2%)
    all_to_all x1, blocking collectives, shards(): gathered = lax.all_to_all(message, STRIPS, 0, 0, tiled=True)  14.6 us
    all_to_all x1, blocking collectives, shards(): lax.all_to_all(jnp.broadcast_to(piece, (group,) + piece.shape), ('y', 'c'...  10.6 us
    all_to_all x1, starting transfers between devices, scatter(): lax.all_to_all(slab.reshape(group, rows, lanes), ('y', 'c'), 0, 0, tiled=...  10.3 us
    all_to_all x1, blocking collectives, shards(): lax.all_to_all(jnp.broadcast_to(total, (group,) + total.shape), ('y', 'c'...  10.1 us
    all_to_all x1, blocking collectives, shards(): lax.all_to_all(partial.reshape(group, cells // group, lanes), ('y', 'c'),...  9.48 us
    ppermute x1, starting transfers between devices, shards(): total = total + lax.ppermute(total, 'zh', PAIRS_ONE)  7.91 us
    ppermute x1, starting transfers between devices, shards(): total = total + lax.ppermute(total, 'zh', PAIRS_TWO)  5.62 us
    all_to_all x1, waiting for transfers between devices, scatter(): lax.all_to_all(slab.reshape(group, rows, lanes), ('y', 'c'), 0, 0, tiled=...  2.91 us
  transfers between devices with their start and end apart: 6, of which 4 were waited for; matrix products, arithmetic and copies ran while one was open for 0% of the time, Pallas kernels for 0%

profile of v2, /device:TPU:1, one launch (start us, length us, event | category | flops | bytes accessed | tf_op | source)
XLA Modules:
  0.0 85.8 jit_solution(17158221338643053355)
XLA Ops:
  1.3 0.0 copy-start
  1.3 15.2 %conditional.2 = (f32[16,128]{1,0:T(8,128)S(1)}) conditional(s32[]{:T(128)} %convert_element_type.3, f32[1,128,128]{2,1,0:T(8,128)} %param.10, (f32[1,128,128]{2,1,0:T(8,128)}, s32[]{:T(128)}) %tuple.26), branch_computations={%region_0.1_spmd, %region_1.2_spmd} | conditional | flops 14 | bytes 213179 | solution.py:322
  1.3 10.3 %all-to-all-start = ((f32[8,16,128]{2,1,0:T(8,128)}), f32[8,16,128]{2,1,0:T(8,128)S(1)}, u32[]{:S(2)}, u32[]{:S(2)}) async-start(f32[8,16,128]{2,1,0:T(8,128)} %bitcast.19), calls=%async_computation | async-start | bytes 131072 | tf_op jit(solution)/shard_map/cond/branch_1_fun/all_to_all | solution.py:319
  13.6 2.9 %all-to-all-done = f32[8,16,128]{2,1,0:T(8,128)S(1)} async-done(((f32[8,16,128]{2,1,0:T(8,128)}), f32[8,16,128]{2,1,0:T(8,128)S(1)}, u32[]{:S(2)}, u32[]{:S(2)}) %all-to-all-start) | async-done | bytes 65568 | tf_op jit(solution)/shard_map/cond/branch_1_fun/all_to_all | solution.py:319
  16.5 4.7 %conditional.3 = (f32[16,128]{1,0:T(8,128)S(1)}) conditional(s32[]{:T(128)} %clamp.3, (s32[]{:T(128)}, f32[16,128]{1,0:T(8,128)S(1)}) %tuple.27, (s32[]{:T(128)}, f32[16,128]{1,0:T(8,128)S(1)}) %tuple.27, (s32[]{:T(128)}, f32[16,128]{1,0:T(8,128)S(1)}) %tuple.27, (s32[]{:T(128)}, f32[16,128]{1,0:T(8,128)S(1)}) %tuple.27), branch_computations={%region_2.3_spmd, %region_3.4_spmd, %region_4.5_spmd, %region_5.6_... | conditional | flops 6145 | bytes 139402 | solution.py:289
  16.5 1.3 %collective-permute-start.2 = (f32[16,128]{1,0:T(8,128)S(1)}, f32[16,128]{1,0:T(8,128)S(1)}, u32[]{:S(2)}, u32[]{:S(2)}) collective-permute-start(f32[16,128]{1,0:T(8,128)S(1)} %get-tuple-element.33), channel_id=1, source_target_pairs={{0,384},{1,385},{2,386},{3,387},{4,388},{5,389},{6,390},{7,391},{8... | collective-permute-start | bytes 24584 | tf_op jit(solution)/shard_map/cond/branch_0_fun/ppermute | solution.py:284
  17.8 1.3 %collective-permute-start.1 = (f32[16,128]{1,0:T(8,128)S(1)}, f32[16,128]{1,0:T(8,128)S(1)}, u32[]{:S(2)}, u32[]{:S(2)}) collective-permute-start(f32[16,128]{1,0:T(8,128)S(1)} %get-tuple-element.33), channel_id=1, source_target_pairs={{0,256},{1,257},{2,258},{3,259},{4,260},{5,261},{6,262},{7,263},{8... | collective-permute-start | bytes 24584 | tf_op jit(solution)/shard_map/cond/branch_0_fun/ppermute | solution.py:282
  19.1 1.3 %collective-permute-start = (f32[16,128]{1,0:T(8,128)S(1)}, f32[16,128]{1,0:T(8,128)S(1)}, u32[]{:S(2)}, u32[]{:S(2)}) collective-permute-start(f32[16,128]{1,0:T(8,128)S(1)} %get-tuple-element.33), channel_id=1, source_target_pairs={{0,128},{1,129},{2,130},{3,131},{4,132},{5,133},{6,134},{7,135},{8... | collective-permute-start | bytes 24584 | tf_op jit(solution)/shard_map/cond/branch_0_fun/ppermute | solution.py:283
  20.4 0.0 collective-permute-done.2
  20.4 0.0 collective-permute-done.1
  20.4 0.7 collective-permute-done
  21.2 10.6 %all_to_all.24 = f32[8,16,128]{2,1,0:T(8,128)S(1)} all-to-all(f32[8,16,128]{2,1,0:T(8,128)S(1)} %broadcast_in_dim.6), channel_id=1, replica_groups=mesh['zh'=4,'y'=4,'c'=2,'zl'=4,'x'=4] {'y','c'}, dimensions={0} | all-to-all | bytes 131072 | tf_op jit(solution)/shard_map/all_to_all | solution.py:326
  31.7 0.0 copy-done
  31.7 0.6 shard_map.51
  32.4 14.6 %all_to_all.25 = f32[16,32,128]{2,1,0:T(8,128)S(1)} all-to-all(f32[16,32,128]{2,1,0:T(8,128)S(1)} %get-tuple-element.47), channel_id=1, replica_groups=mesh['zh'=4,'y'=4,'c'=2,'zl'=4,'x'=4] {'zl','x'}, dimensions={0} | all-to-all | bytes 524288 | tf_op jit(solution)/shard_map/all_to_all | solution.py:340
  47.0 1.3 %shard_map.52 = (f32[2,2,128,128]{3,2,1,0:T(8,128)}, f32[128,128]{1,0:T(8,128)S(1)}) custom-call(s32[1]{0:T(128)} %copy.12.owner_ref, f32[512,128]{1,0:T(8,128)S(1)} %bitcast.14, f32[2,2,16,8,128]{4,3,2,1,0:T(8,128)S(1)} %get-tuple-element.48.screened_ref, f32[2,12,8,128]{3,2,1,0:T(8,128)S(1)} %get-tuple-element.49.scan_ref, f32[1,128,128]{2,1,0:T(8,128)S(1)} %bitcast.16), custom_call_target="tpu_custom_call" | custom-call | tf_op jit(solution)/shard_map/pallas_call | solution.py:293
  48.4 9.5 %all_to_all.26 = f32[8,16,128]{2,1,0:T(8,128)S(1)} all-to-all(f32[8,16,128]{2,1,0:T(8,128)S(1)} %bitcast.17), channel_id=1, replica_groups=mesh['zh'=4,'y'=4,'c'=2,'zl'=4,'x'=4] {'y','c'}, dimensions={0} | all-to-all | bytes 131072 | tf_op jit(solution)/shard_map/all_to_all | solution.py:349
  57.9 7.9 %collective-permute-start.12 = (f32[16,128]{1,0:T(8,128)S(1)}, f32[16,128]{1,0:T(8,128)S(1)}, u32[]{:S(2)}, u32[]{:S(2)}) collective-permute-start(f32[16,128]{1,0:T(8,128)S(1)} %reduce_sum.9), channel_id=1, source_target_pairs={{0,128},{128,0},{256,384},{384,256},{1,129},{129,1},{257,385},{385... | collective-permute-start | bytes 24584 | tf_op jit(solution)/shard_map/ppermute | solution.py:351
  65.8 1.0 %collective-permute-done.12 = f32[16,128]{1,0:T(8,128)S(1)} collective-permute-done((f32[16,128]{1,0:T(8,128)S(1)}, f32[16,128]{1,0:T(8,128)S(1)}, u32[]{:S(2)}, u32[]{:S(2)}) %collective-permute-start.12) | collective-permute-done | bytes 8224 | tf_op jit(solution)/shard_map/ppermute | solution.py:351
  66.8 5.6 %collective-permute-start.13 = (f32[16,128]{1,0:T(8,128)S(1)}, f32[16,128]{1,0:T(8,128)S(1)}, u32[]{:S(2)}, u32[]{:S(2)}) collective-permute-start(f32[16,128]{1,0:T(8,128)S(1)} %add.39), channel_id=1, source_target_pairs={{128,256},{256,128},{384,0},{0,384},{129,257},{257,129},{385,1},{1... | collective-permute-start | bytes 24584 | tf_op jit(solution)/shard_map/ppermute | solution.py:352
  72.4 2.7 %collective-permute-done.13 = f32[16,128]{1,0:T(8,128)S(1)} collective-permute-done((f32[16,128]{1,0:T(8,128)S(1)}, f32[16,128]{1,0:T(8,128)S(1)}, u32[]{:S(2)}, u32[]{:S(2)}) %collective-permute-start.13) | collective-permute-done | bytes 8224 | tf_op jit(solution)/shard_map/ppermute | solution.py:352
  75.1 10.1 %all_to_all.27 = f32[8,16,128]{2,1,0:T(8,128)S(1)} all-to-all(f32[8,16,128]{2,1,0:T(8,128)S(1)} %broadcast_in_dim.7), channel_id=1, replica_groups=mesh['zh'=4,'y'=4,'c'=2,'zl'=4,'x'=4] {'y','c'}, dimensions={0} | all-to-all | bytes 131072 | tf_op jit(solution)/shard_map/all_to_all | solution.py:354
  85.2 0.6 copy.13
  (7 shorter events, 0.0 us)
Async XLA Ops:
  1.3 30.4 %copy-start = (f32[2,2,128,128]{3,2,1,0:T(8,128)S(1)}, f32[2,2,128,128]{3,2,1,0:T(8,128)}, u32[]{:S(2)}) copy-start(f32[2,2,128,128]{3,2,1,0:T(8,128)} %wave_ref.1) | copy-start | bytes 786436
  1.3 15.1 %all-to-all-start = ((f32[8,16,128]{2,1,0:T(8,128)}), f32[8,16,128]{2,1,0:T(8,128)S(1)}, u32[]{:S(2)}, u32[]{:S(2)}) async-start(f32[8,16,128]{2,1,0:T(8,128)} %bitcast.19), calls=%async_computation | async-start | bytes 131072 | tf_op jit(solution)/shard_map/cond/branch_1_fun/all_to_all | solution.py:319
  16.5 3.9 %collective-permute-start.2 = (f32[16,128]{1,0:T(8,128)S(1)}, f32[16,128]{1,0:T(8,128)S(1)}, u32[]{:S(2)}, u32[]{:S(2)}) collective-permute-start(f32[16,128]{1,0:T(8,128)S(1)} %get-tuple-element.33), channel_id=1, source_target_pairs={{0,384},{1,385},{2,386},{3,387},{4,388},{5,389},{6,390},{7,391},{8... | collective-permute-start | bytes 24584 | tf_op jit(solution)/shard_map/cond/branch_0_fun/ppermute | solution.py:284
  17.8 2.6 %collective-permute-start.1 = (f32[16,128]{1,0:T(8,128)S(1)}, f32[16,128]{1,0:T(8,128)S(1)}, u32[]{:S(2)}, u32[]{:S(2)}) collective-permute-start(f32[16,128]{1,0:T(8,128)S(1)} %get-tuple-element.33), channel_id=1, source_target_pairs={{0,256},{1,257},{2,258},{3,259},{4,260},{5,261},{6,262},{7,263},{8... | collective-permute-start | bytes 24584 | tf_op jit(solution)/shard_map/cond/branch_0_fun/ppermute | solution.py:282
  19.1 2.1 %collective-permute-start = (f32[16,128]{1,0:T(8,128)S(1)}, f32[16,128]{1,0:T(8,128)S(1)}, u32[]{:S(2)}, u32[]{:S(2)}) collective-permute-start(f32[16,128]{1,0:T(8,128)S(1)} %get-tuple-element.33), channel_id=1, source_target_pairs={{0,128},{1,129},{2,130},{3,131},{4,132},{5,133},{6,134},{7,135},{8... | collective-permute-start | bytes 24584 | tf_op jit(solution)/shard_map/cond/branch_0_fun/ppermute | solution.py:283
  57.9 9.0 %collective-permute-start.12 = (f32[16,128]{1,0:T(8,128)S(1)}, f32[16,128]{1,0:T(8,128)S(1)}, u32[]{:S(2)}, u32[]{:S(2)}) collective-permute-start(f32[16,128]{1,0:T(8,128)S(1)} %reduce_sum.9), channel_id=1, source_target_pairs={{0,128},{128,0},{256,384},{384,256},{1,129},{129,1},{257,385},{385... | collective-permute-start | bytes 24584 | tf_op jit(solution)/shard_map/ppermute | solution.py:351
  66.8 8.3 %collective-permute-start.13 = (f32[16,128]{1,0:T(8,128)S(1)}, f32[16,128]{1,0:T(8,128)S(1)}, u32[]{:S(2)}, u32[]{:S(2)}) collective-permute-start(f32[16,128]{1,0:T(8,128)S(1)} %add.39), channel_id=1, source_target_pairs={{128,256},{256,128},{384,0},{0,384},{129,257},{257,129},{385,1},{1... | collective-permute-start | bytes 24584 | tf_op jit(solution)/shard_map/ppermute | solution.py:352

commit v3 on v2

--- a/solution.py
+++ b/solution.py
@@ -253,27 +253,7 @@
         image_ref[pl.ds(t, SEGMENTS, stride=steps), :] = image
 
 
-def tree(axes, index, count, source, value):
-    place, core = source
-
-    def pair(a, b):
-        return ((a % count) * CC + core, (b % count) * CC + core)
-
-    up = lax.ppermute(value, axes, [pair(place, place + 1)])
-    far = lax.ppermute(up, axes, [pair(place + 1, place + 2)])
-    down = lax.ppermute(value, axes, [pair(place, place - 1)])
-    return jnp.where(index == place, value, up + far + down)
-
-
-def spread(value, axis, count, place, core):
-    index = lax.axis_index(axis)
-    branches = [
-        functools.partial(tree, (axis, "c"), index, count, (p, c)) for p in range(count) for c in range(CC)
-    ]
-    return lax.switch(place * CC + core, branches, value)
-
-
-def spread_plain(value, axis, count, place):
+def spread(value, axis, count, place):
     index = lax.axis_index(axis)
 
     def branch(p):
@@ -312,20 +292,20 @@
     struct = lambda *shape: jax.ShapeDtypeStruct(shape, jnp.float32)
     own = owner[0]
     core = own % CC
-    group, rows = YY * CC, cells // (YY * CC)
-    home = own // group
-
-    def scatter(slab):
-        parts = lax.all_to_all(slab.reshape(group, rows, lanes), ("y", "c"), 0, 0, tiled=True)
-        return lax.dynamic_index_in_dim(parts, own % group, 0, keepdims=False)
+    group, half = YY * CC, cells // CC
+    home, line = own // group, (own // CC) % YY
+    at_home = lax.axis_index("zh") == home
+
+    def share(slab):
+        both = lax.all_gather(slab, "c", axis=0)
+        return lax.dynamic_slice(both, (core, lax.axis_index("c") * half, 0), (1, half, lanes))[0]
 
     piece = lax.cond(
-        lax.axis_index("zh") == home, scatter, lambda slab: slab[:rows], velocity_bank[0]
-    )
-    piece = spread_plain(piece, "zh", ZH, own // group)
-    velocity = lax.all_to_all(
-        jnp.broadcast_to(piece, (group,) + piece.shape), ("y", "c"), 0, 0, tiled=True
-    ).reshape(1, cells, lanes)
+        at_home & (lax.axis_index("y") == line), share, lambda slab: slab[:half], velocity_bank[0]
+    )
+    piece = lax.cond(at_home, lambda x: spread(x, "y", YY, line), lambda x: x, piece)
+    piece = spread(piece, "zh", ZH, home)
+    velocity = lax.all_gather(piece, "c", axis=0, tiled=True).reshape(1, cells, lanes)
     screened, scan, message = strip_call(
         functools.partial(forward_kernel, freq_total),
         [
@@ -345,15 +325,16 @@
         1,
         (owner, gathered.reshape(N_STRIPS * MESSAGE, lanes), screened, scan, velocity),
     )
-    group = YY * CC
-    pieces = lax.all_to_all(partial.reshape(group, cells // group, lanes), ("y", "c"), 0, 0, tiled=True)
-    total = jnp.sum(pieces, axis=0)
+    both = lax.all_gather(partial, "c", axis=0)
+    begin = lax.axis_index("c") * half
+    total = jnp.sum(lax.dynamic_slice(both, (0, begin, 0), (CC, half, lanes)), axis=0)
+    total = jnp.sum(
+        lax.all_to_all(jnp.broadcast_to(total, (YY, half, lanes)), "y", 0, 0, tiled=True), axis=0
+    )
     total = total + lax.ppermute(total, "zh", PAIRS_ONE)
     total = total + lax.ppermute(total, "zh", PAIRS_TWO)
     total = total * (1.0 / math.sqrt(freq_total))
-    image = lax.all_to_all(
-        jnp.broadcast_to(total, (group,) + total.shape), ("y", "c"), 0, 0, tiled=True
-    )
+    image = lax.all_gather(total, "c", axis=0, tiled=True)
     return (wave_out, image.reshape(cells, lanes))
 
 

time: 86.3 us -> 81.7 us (0.947)
  waiting for transfers between devices: 7.37 us -> 33.2 us
  blocking collectives: 44.8 us -> 20.8 us
  starting transfers between devices: 27.7 us -> 22.4 us
  loops' own time: 2.02 us -> 0.06 us
    all_to_all x4 -> x1, blocking collectives: 44.8 us -> 8.33 us  [shards(): lax.all_to_all(jnp.broadcast_to(total, (YY, half, lanes)), 'y', 0, 0, til...]
    ppermute x1, waiting for transfers between devices: 0.01 us -> 16 us  [run(): down = lax.ppermute(x, axis, [(p, at(p - 1))])]
    all_gather x0 -> x3, blocking collectives: none -> 12.4 us  [the longest x1 5.31 us: shards(): image = lax.all_gather(total, 'c', axis=0, tiled=True)]
    all_to_all x1, waiting for transfers between devices: 2.91 us -> 9.93 us  [shards(): gathered = lax.all_to_all(message, STRIPS, 0, 0, tiled=True)]
    ppermute x1, waiting for transfers between devices: 1.04 us -> 5.3 us  [shards(): total = total + lax.ppermute(total, 'zh', PAIRS_ONE)]
    ppermute x1, starting transfers between devices: 7.91 us -> 4.31 us  [shards(): total = total + lax.ppermute(total, 'zh', PAIRS_ONE)]
    all_to_all x1, starting transfers between devices: 10.3 us -> 8.13 us  [shards(): gathered = lax.all_to_all(message, STRIPS, 0, 0, tiled=True)]
    another operation x2 -> x3, loops' own time: 2.02 us -> 0.06 us  [the longest x1 0.06 us: spread(): return lax.switch(place, [branch(p) for p in range(count)], value)]
where the time goes in v3:
time: 81.7 us; the launch traced here: 81.3 us
  waiting for transfers between devices  33.2 us (41%)
  starting transfers between devices  22.4 us (27%)
  blocking collectives  20.8 us (25%)
  Pallas kernels  2.68 us (3%)
  between operations  1.43 us (2%)
    ppermute x1, waiting for transfers between devices, run(): down = lax.ppermute(x, axis, [(p, at(p - 1))])  16 us
    all_to_all x1, waiting for transfers between devices, shards(): gathered = lax.all_to_all(message, STRIPS, 0, 0, tiled=True)  9.93 us
    all_to_all x1, blocking collectives, shards(): lax.all_to_all(jnp.broadcast_to(total, (YY, half, lanes)), 'y', 0, 0, til...  8.33 us
    all_to_all x1, starting transfers between devices, shards(): gathered = lax.all_to_all(message, STRIPS, 0, 0, tiled=True)  8.13 us
    ppermute x1, starting transfers between devices, shards(): total = total + lax.ppermute(total, 'zh', PAIRS_TWO)  7.23 us
    all_gather x1, blocking collectives, shards(): image = lax.all_gather(total, 'c', axis=0, tiled=True)  5.31 us
    ppermute x1, waiting for transfers between devices, shards(): total = total + lax.ppermute(total, 'zh', PAIRS_ONE)  5.3 us
    ppermute x1, starting transfers between devices, shards(): total = total + lax.ppermute(total, 'zh', PAIRS_ONE)  4.31 us
  transfers between devices with their start and end apart: 6, of which 4 were waited for; matrix products, arithmetic and copies ran while one was open for 0% of the time, Pallas kernels for 0%

profile of v3, /device:TPU:1, one launch (start us, length us, event | category | flops | bytes accessed | tf_op | source)
XLA Modules:
  0.0 81.3 jit_solution(6812028737090388214)
XLA Ops:
  0.6 0.0 copy-start.1
  1.4 0.1 copy-done.1
  1.5 0.0 copy-start
  1.5 18.8 %conditional.6 = (f32[64,128]{1,0:T(8,128)S(1)}) conditional(s32[]{:T(128)} %clamp.6, (s32[]{:T(128)}, f32[64,128]{1,0:T(8,128)S(1)}) %tuple.46, (s32[]{:T(128)}, f32[64,128]{1,0:T(8,128)S(1)}) %tuple.46, (s32[]{:T(128)}, f32[64,128]{1,0:T(8,128)S(1)}) %tuple.46, (s32[]{:T(128)}, f32[64,128]{1,0:T(8,128)S(1)}) %tuple.46), branch_computations={%region_8.9_spmd, %region_9.10_spmd, %region_10.11_spmd, %region_1... | conditional | flops 24577 | bytes 557194 | solution.py:269
  1.5 1.4 %collective-permute-start.17 = (f32[64,128]{1,0:T(8,128)S(1)}, f32[64,128]{1,0:T(8,128)S(1)}, u32[]{:S(2)}, u32[]{:S(2)}) collective-permute-start(f32[64,128]{1,0:T(8,128)S(1)} %get-tuple-element.73), channel_id=1, source_target_pairs={{128,0},{129,1},{130,2},{131,3},{132,4},{133,5},{134,6},{135,7},{1... | collective-permute-start | bytes 98312 | tf_op jit(solution)/shard_map/cond/branch_1_fun/ppermute | solution.py:264
  2.9 0.7 collective-permute-start.16
  3.6 0.7 collective-permute-start.15
  4.3 16.0 %collective-permute-done.17 = f32[64,128]{1,0:T(8,128)S(1)} collective-permute-done((f32[64,128]{1,0:T(8,128)S(1)}, f32[64,128]{1,0:T(8,128)S(1)}, u32[]{:S(2)}, u32[]{:S(2)}) %collective-permute-start.17) | collective-permute-done | bytes 32800 | tf_op jit(solution)/shard_map/cond/branch_1_fun/ppermute | solution.py:264
  20.3 0.0 collective-permute-done.16
  20.3 0.0 collective-permute-done.15
  20.3 3.9 %all_gather.15 = f32[128,128]{1,0:T(8,128)S(1)} all-gather(f32[64,128]{1,0:T(8,128)S(1)} %get-tuple-element.107), channel_id=1, replica_groups=mesh['zh'=4,'y'=4,'c'=2,'zl'=4,'x'=4] {'c'}, dimensions={0}, use_global_device_ids=true | all-gather | bytes 98304 | tf_op jit(solution)/shard_map/all_gather | solution.py:308
  24.2 0.0 copy-done
  24.2 1.3 %shard_map.50 = (f32[2,2,16,8,128]{4,3,2,1,0:T(8,128)S(1)}, f32[2,12,8,128]{3,2,1,0:T(8,128)S(1)}, f32[16,32,128]{2,1,0:T(8,128)}) custom-call(s32[1]{0:T(128)} %copy.18.owner_ref, f32[2,2,128,128]{3,2,1,0:T(8,128)S(1)} %copy-done, f32[1,128,128]{2,1,0:T(8,128)S(1)} %bitcast.13), custom_call_target="tpu_custom_call" | custom-call | tf_op jit(solution)/shard_map/pallas_call | solution.py:273
  25.6 8.1 %all-to-all-start = ((f32[16,32,128]{2,1,0:T(8,128)}), f32[16,32,128]{2,1,0:T(8,128)S(1)}, u32[]{:S(2)}, u32[]{:S(2)}) async-start(f32[16,32,128]{2,1,0:T(8,128)} %get-tuple-element.85), calls=%async_computation | async-start | bytes 524288 | tf_op jit(solution)/shard_map/all_to_all | solution.py:320
  33.7 9.9 %all-to-all-done = f32[16,32,128]{2,1,0:T(8,128)S(1)} async-done(((f32[16,32,128]{2,1,0:T(8,128)}), f32[16,32,128]{2,1,0:T(8,128)S(1)}, u32[]{:S(2)}, u32[]{:S(2)}) %all-to-all-start) | async-done | bytes 262176 | tf_op jit(solution)/shard_map/all_to_all | solution.py:320
  43.7 1.3 %shard_map.51 = (f32[2,2,128,128]{3,2,1,0:T(8,128)}, f32[128,128]{1,0:T(8,128)S(1)}) custom-call(s32[1]{0:T(128)} %copy.18.owner_ref, f32[512,128]{1,0:T(8,128)S(1)} %bitcast.12, f32[2,2,16,8,128]{4,3,2,1,0:T(8,128)S(1)} %get-tuple-element.86.screened_ref, f32[2,12,8,128]{3,2,1,0:T(8,128)S(1)} %get-tuple-element.87.scan_ref, f32[1,128,128]{2,1,0:T(8,128)S(1)} %bitcast.14), custom_call_target="tpu_custom_call" | custom-call | tf_op jit(solution)/shard_map/pallas_call | solution.py:273
  45.0 3.2 %all-gather = f32[256,128]{1,0:T(8,128)S(1)} all-gather(f32[128,128]{1,0:T(8,128)S(1)} %get-tuple-element.89), channel_id=2, replica_groups=mesh['zh'=4,'y'=4,'c'=2,'zl'=4,'x'=4] {'c'}, dimensions={0}, use_global_device_ids=true | all-gather | bytes 196608 | tf_op jit(solution)/shard_map/all_gather | solution.py:328
  48.2 8.3 %all_to_all.10 = f32[4,64,128]{2,1,0:T(8,128)S(1)} all-to-all(f32[4,64,128]{2,1,0:T(8,128)S(1)} %broadcast_in_dim.3), channel_id=1, replica_groups=mesh['zh'=4,'y'=4,'c'=2,'zl'=4,'x'=4] {'y'}, dimensions={0} | all-to-all | bytes 262144 | tf_op jit(solution)/shard_map/all_to_all | solution.py:332
  56.6 4.3 %collective-permute-start.24 = (f32[64,128]{1,0:T(8,128)S(1)}, f32[64,128]{1,0:T(8,128)S(1)}, u32[]{:S(2)}, u32[]{:S(2)}) collective-permute-start(f32[64,128]{1,0:T(8,128)S(1)} %reduce_sum.19), channel_id=1, source_target_pairs={{0,128},{128,0},{256,384},{384,256},{1,129},{129,1},{257,385},{385... | collective-permute-start | bytes 98312 | tf_op jit(solution)/shard_map/ppermute | solution.py:334
  60.9 5.3 %collective-permute-done.24 = f32[64,128]{1,0:T(8,128)S(1)} collective-permute-done((f32[64,128]{1,0:T(8,128)S(1)}, f32[64,128]{1,0:T(8,128)S(1)}, u32[]{:S(2)}, u32[]{:S(2)}) %collective-permute-start.24) | collective-permute-done | bytes 32800 | tf_op jit(solution)/shard_map/ppermute | solution.py:334
  66.2 7.2 %collective-permute-start.25 = (f32[64,128]{1,0:T(8,128)S(1)}, f32[64,128]{1,0:T(8,128)S(1)}, u32[]{:S(2)}, u32[]{:S(2)}) collective-permute-start(f32[64,128]{1,0:T(8,128)S(1)} %add.75), channel_id=1, source_target_pairs={{128,256},{256,128},{384,0},{0,384},{129,257},{257,129},{385,1},{1... | collective-permute-start | bytes 98312 | tf_op jit(solution)/shard_map/ppermute | solution.py:335
  73.5 1.9 %collective-permute-done.25 = f32[64,128]{1,0:T(8,128)S(1)} collective-permute-done((f32[64,128]{1,0:T(8,128)S(1)}, f32[64,128]{1,0:T(8,128)S(1)}, u32[]{:S(2)}, u32[]{:S(2)}) %collective-permute-start.25) | collective-permute-done | bytes 32800 | tf_op jit(solution)/shard_map/ppermute | solution.py:335
  75.4 5.3 %all_gather.18 = f32[128,128]{1,0:T(8,128)S(1)} all-gather(f32[64,128]{1,0:T(8,128)S(1)} %add_multiply_fusion), channel_id=1, replica_groups=mesh['zh'=4,'y'=4,'c'=2,'zl'=4,'x'=4] {'c'}, dimensions={0}, use_global_device_ids=true | all-gather | bytes 98304 | tf_op jit(solution)/shard_map/all_gather | solution.py:337
  80.7 0.6 copy.19
  (9 shorter events, 0.1 us)
Async XLA Ops:
  0.6 0.8 %copy-start.1 = (f32[1,128,128]{2,1,0:T(8,128)S(1)}, f32[1,128,128]{2,1,0:T(8,128)}, u32[]{:S(2)}) copy-start(f32[1,128,128]{2,1,0:T(8,128)} %param.16) | copy-start | bytes 196612
  1.5 22.8 %copy-start = (f32[2,2,128,128]{3,2,1,0:T(8,128)S(1)}, f32[2,2,128,128]{3,2,1,0:T(8,128)}, u32[]{:S(2)}) copy-start(f32[2,2,128,128]{3,2,1,0:T(8,128)} %wave_ref.1) | copy-start | bytes 786436
  1.5 18.8 %collective-permute-start.17 = (f32[64,128]{1,0:T(8,128)S(1)}, f32[64,128]{1,0:T(8,128)S(1)}, u32[]{:S(2)}, u32[]{:S(2)}) collective-permute-start(f32[64,128]{1,0:T(8,128)S(1)} %get-tuple-element.73), channel_id=1, source_target_pairs={{128,0},{129,1},{130,2},{131,3},{132,4},{133,5},{134,6},{135,7},{1... | collective-permute-start | bytes 98312 | tf_op jit(solution)/shard_map/cond/branch_1_fun/ppermute | solution.py:264
  2.9 17.4 %collective-permute-start.16 = (f32[64,128]{1,0:T(8,128)S(1)}, f32[64,128]{1,0:T(8,128)S(1)}, u32[]{:S(2)}, u32[]{:S(2)}) collective-permute-start(f32[64,128]{1,0:T(8,128)S(1)} %get-tuple-element.73), channel_id=1, source_target_pairs={{128,384},{129,385},{130,386},{131,387},{132,388},{133,389},{134,3... | collective-permute-start | bytes 98312 | tf_op jit(solution)/shard_map/cond/branch_1_fun/ppermute | solution.py:262
  3.6 16.7 %collective-permute-start.15 = (f32[64,128]{1,0:T(8,128)S(1)}, f32[64,128]{1,0:T(8,128)S(1)}, u32[]{:S(2)}, u32[]{:S(2)}) collective-permute-start(f32[64,128]{1,0:T(8,128)S(1)} %get-tuple-element.73), channel_id=1, source_target_pairs={{128,256},{129,257},{130,258},{131,259},{132,260},{133,261},{134,2... | collective-permute-start | bytes 98312 | tf_op jit(solution)/shard_map/cond/branch_1_fun/ppermute | solution.py:263
  25.6 18.1 %all-to-all-start = ((f32[16,32,128]{2,1,0:T(8,128)}), f32[16,32,128]{2,1,0:T(8,128)S(1)}, u32[]{:S(2)}, u32[]{:S(2)}) async-start(f32[16,32,128]{2,1,0:T(8,128)} %get-tuple-element.85), calls=%async_computation | async-start | bytes 524288 | tf_op jit(solution)/shard_map/all_to_all | solution.py:320
  56.6 9.6 %collective-permute-start.24 = (f32[64,128]{1,0:T(8,128)S(1)}, f32[64,128]{1,0:T(8,128)S(1)}, u32[]{:S(2)}, u32[]{:S(2)}) collective-permute-start(f32[64,128]{1,0:T(8,128)S(1)} %reduce_sum.19), channel_id=1, source_target_pairs={{0,128},{128,0},{256,384},{384,256},{1,129},{129,1},{257,385},{385... | collective-permute-start | bytes 98312 | tf_op jit(solution)/shard_map/ppermute | solution.py:334
  66.2 9.1 %collective-permute-start.25 = (f32[64,128]{1,0:T(8,128)S(1)}, f32[64,128]{1,0:T(8,128)S(1)}, u32[]{:S(2)}, u32[]{:S(2)}) collective-permute-start(f32[64,128]{1,0:T(8,128)S(1)} %add.75), channel_id=1, source_target_pairs={{128,256},{256,128},{384,0},{0,384},{129,257},{257,129},{385,1},{1... | collective-permute-start | bytes 98312 | tf_op jit(solution)/shard_map/ppermute | solution.py:335

commit v4 on v3

--- a/solution.py
+++ b/solution.py
@@ -92,7 +92,7 @@
     return mul(scale(2.0, eps), add(here, scale(BETA, lap)))
 
 
-def forward_kernel(freq_total, owner_ref, wave_ref, vel_ref, screened_ref, scan_ref, message_ref, rows_ref):
+def forward_kernel(freq_total, owner_ref, wave_ref, vel_ref, screened_ref, scan_ref, message_ref):
     freq_local, cells = wave_ref.shape[1], wave_ref.shape[2]
     steps = cells // SEGMENTS
     lanes = wave_ref.shape[3]
@@ -114,7 +114,7 @@
             screened_ref[f, 0, t] = re * cos - im * sin
             screened_ref[f, 1, t] = re * sin + im * cos
 
-    rows_ref[...] = jnp.zeros(rows_ref.shape, jnp.float32)
+    message_ref[...] = jnp.zeros(message_ref.shape, jnp.float32)
     for f in range(freq_local):
         wave = lambda t: (screened_ref[f, 0, t], screened_ref[f, 1, t])
         state = [[(one, zero), (zero, zero)], [(zero, zero), (one, zero)], [(zero, zero), (zero, zero)]]
@@ -157,22 +157,17 @@
         base = f * FIELDS * 2
         for i, q in enumerate(fields):
             for c in range(2):
-                rows_ref[base + 2 * i + c : base + 2 * i + c + 1, :] = q[c][SEGMENTS - 1 :, :]
+                message_ref[base + 2 * i + c : base + 2 * i + c + 1, :] = q[c][SEGMENTS - 1 :, :]
         for c in range(2):
-            rows_ref[base + 10 + c : base + 11 + c, :] = screened_ref[f, c, 0][0:1, :]
-            rows_ref[base + 12 + c : base + 13 + c, :] = screened_ref[f, c, steps - 1][SEGMENTS - 1 :, :]
+            message_ref[base + 10 + c : base + 11 + c, :] = screened_ref[f, c, 0][0:1, :]
+            message_ref[base + 12 + c : base + 13 + c, :] = screened_ref[f, c, steps - 1][SEGMENTS - 1 :, :]
     tail = freq_local * FIELDS * 2
-    rows_ref[tail : tail + 1, :] = velocity(0)[0:1, :]
-    rows_ref[tail + 1 : tail + 2, :] = velocity(steps - 1)[SEGMENTS - 1 :, :]
-    whole = rows_ref[...]
-    for s in range(message_ref.shape[0]):
-        message_ref[s] = whole
+    message_ref[tail : tail + 1, :] = velocity(0)[0:1, :]
+    message_ref[tail + 1 : tail + 2, :] = velocity(steps - 1)[SEGMENTS - 1 :, :]
 
 
 def backward_kernel(freq_total, owner_ref, gathered_ref, screened_ref, scan_ref, vel_ref, out_ref, image_ref, pick_ref):
-    freq_local, cells = out_ref.shape[1], out_ref.shape[2]
-    steps = cells // SEGMENTS
-    lanes = out_ref.shape[3]
+    freq_local, steps, _, lanes = out_ref.shape[1:]
     strips = gathered_ref.shape[0] // MESSAGE
     core = 0
     strip = lax.axis_index("zl") * XX + lax.axis_index("x")
@@ -243,8 +238,8 @@
             wave = lambda t: (screened_ref[f, 0, t], screened_ref[f, 1, t])
             w, d = state[f]
             out = sub(w, wave(t))
-            out_ref[0, f, pl.ds(t, SEGMENTS, stride=steps), :] = out[0]
-            out_ref[1, f, pl.ds(t, SEGMENTS, stride=steps), :] = out[1]
+            out_ref[0, f, t] = out[0]
+            out_ref[1, f, t] = out[1]
             image = out[0] if image is None else image + out[0]
             if t < steps - 1:
                 eps = inverse_kappa(vel, omegas[f])
@@ -311,16 +306,17 @@
         [
             struct(freq_local, 2, steps, SEGMENTS, lanes),
             struct(freq_local, 12, SEGMENTS, lanes),
-            struct(N_STRIPS, MESSAGE, lanes),
+            struct(MESSAGE, lanes),
         ],
-        [pltpu.VMEM((MESSAGE, lanes), jnp.float32)],
+        [],
         1,
         (owner, wavefield, velocity),
     )
+    message = jnp.broadcast_to(message, (N_STRIPS, MESSAGE, lanes))
     gathered = lax.all_to_all(message, STRIPS, 0, 0, tiled=True)
     wave_out, partial = strip_call(
         functools.partial(backward_kernel, freq_total),
-        [struct(2, freq_local, cells, lanes), struct(cells, lanes)],
+        [struct(2, freq_local, steps, SEGMENTS, lanes), struct(cells, lanes)],
         [pltpu.VMEM((4 * freq_local, N_STRIPS, lanes), jnp.float32)],
         1,
         (owner, gathered.reshape(N_STRIPS * MESSAGE, lanes), screened, scan, velocity),
@@ -335,6 +331,7 @@
     total = total + lax.ppermute(total, "zh", PAIRS_TWO)
     total = total * (1.0 / math.sqrt(freq_total))
     image = lax.all_gather(total, "c", axis=0, tiled=True)
+    wave_out = jnp.swapaxes(wave_out, 2, 3).reshape(wavefield.shape)
     return (wave_out, image.reshape(cells, lanes))
 
 

time: 81.7 us -> 85.8 us (1.050)
  waiting for transfers between devices: 33.2 us -> 41.2 us
  starting transfers between devices: 22.4 us -> 16.7 us
  blocking collectives: 20.8 us -> 22.5 us
  Pallas kernels: 2.68 us -> 1.19 us
  local copies, waits for them, and re-layouts: 0.73 us -> 2.21 us
    ppermute x1, waiting for transfers between devices: 0.01 us -> 20.3 us  [run(): up = lax.ppermute(x, axis, [(p, at(p + 1))])]
    ppermute x1, waiting for transfers between devices: 16 us -> 0.01 us  [run(): down = lax.ppermute(x, axis, [(p, at(p - 1))])]
    ppermute x1, starting transfers between devices: 7.23 us -> 1.91 us  [shards(): total = total + lax.ppermute(total, 'zh', PAIRS_TWO)]
    ppermute x1, waiting for transfers between devices: 1.89 us -> 5.89 us  [shards(): total = total + lax.ppermute(total, 'zh', PAIRS_TWO)]
    all_to_all x1, blocking collectives: 8.33 us -> 10.3 us  [shards(): lax.all_to_all(jnp.broadcast_to(total, (YY, half, lanes)), 'y', 0, 0, til...]
    pallas_call x2, Pallas kernels: 2.68 us -> 1.19 us  [strip_call(): pl.pallas_call(kernel, out_shape=outs, in_specs=[pl.BlockSpec(memory_spac...]
  transfers between devices with their start and end apart: 6 -> 6, of which waited for: 4 -> 4; matrix products, arithmetic and copies ran while one was open for 0% -> 1% of each run, Pallas kernels for 0% -> 0%
where the time goes in v4:
time: 85.8 us; the launch traced here: 85.4 us
  waiting for transfers between devices  41.2 us (48%)
  blocking collectives  22.5 us (26%)
  starting transfers between devices  16.7 us (19%)
  local copies, waits for them, and re-layouts  2.21 us (3%)
  between operations  1.44 us (2%)
  Pallas kernels  1.19 us (1%)
    ppermute x1, waiting for transfers between devices, run(): up = lax.ppermute(x, axis, [(p, at(p + 1))])  20.3 us
    all_to_all x1, blocking collectives, shards(): lax.all_to_all(jnp.broadcast_to(total, (YY, half, lanes)), 'y', 0, 0, til...  10.3 us
    all_to_all x1, waiting for transfers between devices, shards(): gathered = lax.all_to_all(message, STRIPS, 0, 0, tiled=True)  9.93 us
    all_to_all x1, starting transfers between devices, shards(): gathered = lax.all_to_all(message, STRIPS, 0, 0, tiled=True)  7.52 us
    ppermute x1, waiting for transfers between devices, shards(): total = total + lax.ppermute(total, 'zh', PAIRS_TWO)  5.89 us
    all_gather x1, blocking collectives, shards(): image = lax.all_gather(total, 'c', axis=0, tiled=True)  5.57 us
    ppermute x1, waiting for transfers between devices, shards(): total = total + lax.ppermute(total, 'zh', PAIRS_ONE)  5.08 us
    ppermute x1, starting transfers between devices, shards(): total = total + lax.ppermute(total, 'zh', PAIRS_ONE)  4.53 us
  transfers between devices with their start and end apart: 6, of which 4 were waited for; matrix products, arithmetic and copies ran while one was open for 1% of the time, Pallas kernels for 0%

profile of v4, /device:TPU:1, one launch (start us, length us, event | category | flops | bytes accessed | tf_op | source)
XLA Modules:
  0.0 85.4 jit_solution(14646629898339262344)
XLA Ops:
  0.6 0.0 copy-start.1
  1.4 0.1 copy-done.1
  1.5 0.0 copy-start
  1.5 23.1 %conditional.6 = (f32[64,128]{1,0:T(8,128)S(1)}) conditional(s32[]{:T(128)} %clamp.6, (s32[]{:T(128)}, f32[64,128]{1,0:T(8,128)S(1)}) %tuple.46, (s32[]{:T(128)}, f32[64,128]{1,0:T(8,128)S(1)}) %tuple.46, (s32[]{:T(128)}, f32[64,128]{1,0:T(8,128)S(1)}) %tuple.46, (s32[]{:T(128)}, f32[64,128]{1,0:T(8,128)S(1)}) %tuple.46), branch_computations={%region_8.9_spmd, %region_9.10_spmd, %region_10.11_spmd, %region_1... | conditional | flops 24577 | bytes 557194 | solution.py:264
  1.5 0.8 collective-permute-start.23
  2.3 0.7 collective-permute-start.22
  3.0 1.3 %collective-permute-start.21 = (f32[64,128]{1,0:T(8,128)S(1)}, f32[64,128]{1,0:T(8,128)S(1)}, u32[]{:S(2)}, u32[]{:S(2)}) collective-permute-start(f32[64,128]{1,0:T(8,128)S(1)} %get-tuple-element.77), channel_id=1, source_target_pairs={{384,0},{385,1},{386,2},{387,3},{388,4},{389,5},{390,6},{391,7},{3... | collective-permute-start | bytes 98312 | tf_op jit(solution)/shard_map/cond/branch_3_fun/ppermute | solution.py:258
  4.3 0.0 collective-permute-done.23
  4.3 0.0 collective-permute-done.22
  4.3 20.3 %collective-permute-done.21 = f32[64,128]{1,0:T(8,128)S(1)} collective-permute-done((f32[64,128]{1,0:T(8,128)S(1)}, f32[64,128]{1,0:T(8,128)S(1)}, u32[]{:S(2)}, u32[]{:S(2)}) %collective-permute-start.21) | collective-permute-done | bytes 32800 | tf_op jit(solution)/shard_map/cond/branch_3_fun/ppermute | solution.py:258
  24.6 3.4 %all_gather.15 = f32[128,128]{1,0:T(8,128)S(1)} all-gather(f32[64,128]{1,0:T(8,128)S(1)} %get-tuple-element.107), channel_id=1, replica_groups=mesh['zh'=4,'y'=4,'c'=2,'zl'=4,'x'=4] {'c'}, dimensions={0}, use_global_device_ids=true | all-gather | bytes 98304 | tf_op jit(solution)/shard_map/all_gather | solution.py:303
  28.0 0.0 copy-done
  28.0 0.6 shard_map.50
  28.6 0.7 broadcast_in_dim.6
  29.4 7.5 %all-to-all-start = ((f32[16,32,128]{2,1,0:T(8,128)}), f32[16,32,128]{2,1,0:T(8,128)S(1)}, u32[]{:S(2)}, u32[]{:S(2)}) async-start(f32[16,32,128]{2,1,0:T(8,128)} %broadcast_in_dim.6), calls=%async_computation | async-start | bytes 524288 | tf_op jit(solution)/shard_map/all_to_all | solution.py:316
  36.9 9.9 %all-to-all-done = f32[16,32,128]{2,1,0:T(8,128)S(1)} async-done(((f32[16,32,128]{2,1,0:T(8,128)}), f32[16,32,128]{2,1,0:T(8,128)S(1)}, u32[]{:S(2)}, u32[]{:S(2)}) %all-to-all-start) | async-done | bytes 262176 | tf_op jit(solution)/shard_map/all_to_all | solution.py:316
  46.8 0.6 shard_map.51
  47.4 3.2 %all-gather = f32[256,128]{1,0:T(8,128)S(1)} all-gather(f32[128,128]{1,0:T(8,128)S(1)} %get-tuple-element.89), channel_id=2, replica_groups=mesh['zh'=4,'y'=4,'c'=2,'zl'=4,'x'=4] {'c'}, dimensions={0}, use_global_device_ids=true | all-gather | bytes 196608 | tf_op jit(solution)/shard_map/all_gather | solution.py:324
  50.7 10.3 %all_to_all.10 = f32[4,64,128]{2,1,0:T(8,128)S(1)} all-to-all(f32[4,64,128]{2,1,0:T(8,128)S(1)} %broadcast_in_dim.7), channel_id=1, replica_groups=mesh['zh'=4,'y'=4,'c'=2,'zl'=4,'x'=4] {'y'}, dimensions={0} | all-to-all | bytes 262144 | tf_op jit(solution)/shard_map/all_to_all | solution.py:328
  61.0 4.5 %collective-permute-start.24 = (f32[64,128]{1,0:T(8,128)S(1)}, f32[64,128]{1,0:T(8,128)S(1)}, u32[]{:S(2)}, u32[]{:S(2)}) collective-permute-start(f32[64,128]{1,0:T(8,128)S(1)} %reduce_sum.19), channel_id=1, source_target_pairs={{0,128},{128,0},{256,384},{384,256},{1,129},{129,1},{257,385},{385... | collective-permute-start | bytes 98312 | tf_op jit(solution)/shard_map/ppermute | solution.py:330
  65.5 5.1 %collective-permute-done.24 = f32[64,128]{1,0:T(8,128)S(1)} collective-permute-done((f32[64,128]{1,0:T(8,128)S(1)}, f32[64,128]{1,0:T(8,128)S(1)}, u32[]{:S(2)}, u32[]{:S(2)}) %collective-permute-start.24) | collective-permute-done | bytes 32800 | tf_op jit(solution)/shard_map/ppermute | solution.py:330
  70.6 1.9 %collective-permute-start.25 = (f32[64,128]{1,0:T(8,128)S(1)}, f32[64,128]{1,0:T(8,128)S(1)}, u32[]{:S(2)}, u32[]{:S(2)}) collective-permute-start(f32[64,128]{1,0:T(8,128)S(1)} %add.75), channel_id=1, source_target_pairs={{128,256},{256,128},{384,0},{0,384},{129,257},{257,129},{385,1},{1... | collective-permute-start | bytes 98312 | tf_op jit(solution)/shard_map/ppermute | solution.py:331
  72.5 0.8 copy.7
  73.3 5.9 %collective-permute-done.25 = f32[64,128]{1,0:T(8,128)S(1)} collective-permute-done((f32[64,128]{1,0:T(8,128)S(1)}, f32[64,128]{1,0:T(8,128)S(1)}, u32[]{:S(2)}, u32[]{:S(2)}) %collective-permute-start.25) | collective-permute-done | bytes 32800 | tf_op jit(solution)/shard_map/ppermute | solution.py:331
  79.1 5.6 %all_gather.18 = f32[128,128]{1,0:T(8,128)S(1)} all-gather(f32[64,128]{1,0:T(8,128)S(1)} %add_multiply_fusion), channel_id=1, replica_groups=mesh['zh'=4,'y'=4,'c'=2,'zl'=4,'x'=4] {'c'}, dimensions={0}, use_global_device_ids=true | all-gather | bytes 98304 | tf_op jit(solution)/shard_map/all_gather | solution.py:333
  84.7 0.6 copy.22
  (9 shorter events, 0.1 us)
Async XLA Ops:
  0.6 0.8 copy-start.1
  1.5 26.5 %copy-start = (f32[2,2,128,128]{3,2,1,0:T(8,128)S(1)}, f32[2,2,128,128]{3,2,1,0:T(8,128)}, u32[]{:S(2)}) copy-start(f32[2,2,128,128]{3,2,1,0:T(8,128)} %wave_ref.1) | copy-start | bytes 786436
  1.5 2.8 %collective-permute-start.23 = (f32[64,128]{1,0:T(8,128)S(1)}, f32[64,128]{1,0:T(8,128)S(1)}, u32[]{:S(2)}, u32[]{:S(2)}) collective-permute-start(f32[64,128]{1,0:T(8,128)S(1)} %get-tuple-element.77), channel_id=1, source_target_pairs={{384,256},{385,257},{386,258},{387,259},{388,260},{389,261},{390,2... | collective-permute-start | bytes 98312 | tf_op jit(solution)/shard_map/cond/branch_3_fun/ppermute | solution.py:259
  2.3 2.0 %collective-permute-start.22 = (f32[64,128]{1,0:T(8,128)S(1)}, f32[64,128]{1,0:T(8,128)S(1)}, u32[]{:S(2)}, u32[]{:S(2)}) collective-permute-start(f32[64,128]{1,0:T(8,128)S(1)} %get-tuple-element.77), channel_id=1, source_target_pairs={{384,128},{385,129},{386,130},{387,131},{388,132},{389,133},{390,1... | collective-permute-start | bytes 98312 | tf_op jit(solution)/shard_map/cond/branch_3_fun/ppermute | solution.py:257
  3.0 21.6 %collective-permute-start.21 = (f32[64,128]{1,0:T(8,128)S(1)}, f32[64,128]{1,0:T(8,128)S(1)}, u32[]{:S(2)}, u32[]{:S(2)}) collective-permute-start(f32[64,128]{1,0:T(8,128)S(1)} %get-tuple-element.77), channel_id=1, source_target_pairs={{384,0},{385,1},{386,2},{387,3},{388,4},{389,5},{390,6},{391,7},{3... | collective-permute-start | bytes 98312 | tf_op jit(solution)/shard_map/cond/branch_3_fun/ppermute | solution.py:258
  29.4 17.5 %all-to-all-start = ((f32[16,32,128]{2,1,0:T(8,128)}), f32[16,32,128]{2,1,0:T(8,128)S(1)}, u32[]{:S(2)}, u32[]{:S(2)}) async-start(f32[16,32,128]{2,1,0:T(8,128)} %broadcast_in_dim.6), calls=%async_computation | async-start | bytes 524288 | tf_op jit(solution)/shard_map/all_to_all | solution.py:316
  61.0 9.6 %collective-permute-start.24 = (f32[64,128]{1,0:T(8,128)S(1)}, f32[64,128]{1,0:T(8,128)S(1)}, u32[]{:S(2)}, u32[]{:S(2)}) collective-permute-start(f32[64,128]{1,0:T(8,128)S(1)} %reduce_sum.19), channel_id=1, source_target_pairs={{0,128},{128,0},{256,384},{384,256},{1,129},{129,1},{257,385},{385... | collective-permute-start | bytes 98312 | tf_op jit(solution)/shard_map/ppermute | solution.py:330
  70.6 8.6 %collective-permute-start.25 = (f32[64,128]{1,0:T(8,128)S(1)}, f32[64,128]{1,0:T(8,128)S(1)}, u32[]{:S(2)}, u32[]{:S(2)}) collective-permute-start(f32[64,128]{1,0:T(8,128)S(1)} %add.75), channel_id=1, source_target_pairs={{128,256},{256,128},{384,0},{0,384},{129,257},{257,129},{385,1},{1... | collective-permute-start | bytes 98312 | tf_op jit(solution)/shard_map/ppermute | solution.py:331
